TPU v7x, 512 devices: a whole 4x4x16 slice. The times are simulated.
512 devices in a mesh: pipe: 16 (over z), dp: 32 (over x, y, core).
Axes of the slice: x: 4, y: 4, z: 16, core: 2. Of those that a mesh axis runs over, the one named last changes fastest.
Arguments:
- sent_base: bfloat16 [16, 256, 4096], P('pipe', None, 'dp'), may hold values from -13 to 13, as said below
- sent_part: bfloat16 [16, 256, 4096], P('pipe', None, 'dp'), may hold values from -4 to 4
- cot_base: bfloat16 [16, 256, 4096], P('pipe', None, 'dp'), may hold values from -7 to 7
- cot_part: bfloat16 [16, 256, 4096], P('pipe', None, 'dp'), may hold values from -7 to 7
- norm_gain: bfloat16 [16, 4096], P('pipe', 'dp'), may hold values from 0.25 to 1.75
- up_blocks: bfloat16 [16, 128, 64, 2048], P('pipe', 'dp'), may hold values from -2 to 2, as said below
- down_blocks: bfloat16 [16, 128, 64, 2048], P('pipe', 'dp'), may hold values from -2 to 2, as said below
- up_index: int32 [16, 128, 32], P('pipe', 'dp'), may hold values from 0 to 63, as said below
- down_index: int32 [16, 128, 32], P('pipe', 'dp'), may hold values from 0 to 63, as said below
Outputs:
- out_base: bfloat16 [16, 256, 4096], P('pipe', None, 'dp')
- out_part: bfloat16 [16, 256, 4096], P('pipe', None, 'dp')
- back_base: bfloat16 [16, 256, 4096], P('pipe', None, 'dp')
- back_part: bfloat16 [16, 256, 4096], P('pipe', None, 'dp')
- up_grad: bfloat16 [16, 128, 64, 2048], P('pipe', 'dp')
- down_grad: bfloat16 [16, 128, 64, 2048], P('pipe', 'dp')
- gain_gradient: float32 [16, 4096], P('pipe', 'dp')
Inputs may be any that keep to these rules, and one draw needn't show every extreme that they name: `up_index`: each row of the last dimension lists 32 different block indices in increasing order, so that half of the blocks of each block column of the up projection are kept. `down_index`: each row of the last dimension lists 32 different block indices in increasing order, so that half of the blocks of each block row of the down projection are kept. `sent_base`: token rows of order one. `up_blocks`: entries of standard deviation one over the square root of 2048. `down_blocks`: entries of standard deviation one over the square root of 4096.
All inputs are finite; a program needn't handle non-finite values.
Results may differ from a plain program's by a relative error of at most 0.019.
Values may be sent and summed in bfloat16 or wider, within the bound.
No kernel may reach another device: no remote copies, remote signals or barrier semaphores. Data moves between devices by JAX's collectives and lax.ppermute only.
A program may use at most 128 MiB of HBM per device.

v0:
```python
import jax
import jax.numpy as jnp
from jax import lax
from jax.sharding import PartitionSpec as P

eps = 1e-05


def passed_along(shard, axis, by):
    count = lax.axis_size(axis)
    return lax.ppermute(shard, axis, [(i, (i + by) % count) for i in range(count)])


def place_blocks(values, index, nblk):
    tokens = values.shape[0]
    blk = values.shape[2] // index.shape[1]
    pieces = values.reshape(tokens, index.shape[0] * index.shape[1], blk)
    onehot = (index.reshape(-1)[:, None] == jnp.arange(nblk)[None, :]).astype(jnp.float32)
    spread = jnp.einsum("tmo,mb->tbo", pieces, onehot, precision=lax.Precision.HIGHEST)
    return spread.reshape(tokens, nblk * blk)


def per_device(
    sent_base,
    sent_part,
    cot_base,
    cot_part,
    norm_gain,
    up_blocks,
    down_blocks,
    up_index,
    down_index,
):
    arrived_base, arrived_part = passed_along((sent_base, sent_part), "pipe", 1)
    full_rows, full_gain = (
        lax.all_gather(arrived_base, "dp", axis=2, tiled=True),
        lax.all_gather(norm_gain, "dp", axis=1, tiled=True),
    )
    odd = (lax.axis_index("pipe") % 2).astype(jnp.float32)
    complete_input = full_rows[0].astype(jnp.float32)
    tokens, width = complete_input.shape
    w_up = up_blocks[0]
    w_down = down_blocks[0]
    idx_up = up_index[0]
    idx_down = down_index[0]
    hblk, blk, _ = w_up.shape
    kept = idx_up.shape[1]
    nblk = width // blk
    root_mean_square = jnp.sqrt(
        jnp.mean(complete_input * complete_input, axis=-1, keepdims=True) + eps
    )
    complete_scaled_input = complete_input / root_mean_square
    complete_gain = full_gain[0].astype(jnp.float32)
    normalized_rows = (complete_scaled_input * complete_gain).astype(jnp.bfloat16)
    gathered = normalized_rows.reshape(tokens, nblk, blk)[:, idx_up].reshape(
        tokens, hblk, kept * blk
    )
    pre = jnp.einsum("tcm,com->tco", gathered, w_up, preferred_element_type=jnp.float32)
    hidden = jax.nn.silu(pre).astype(jnp.bfloat16)
    terms = jnp.einsum("tci,cim->tcm", hidden, w_down, preferred_element_type=jnp.float32)
    partial_value = place_blocks(terms, idx_down, nblk)
    share = lax.psum_scatter(
        partial_value.astype(jnp.bfloat16), "dp", scatter_dimension=1, tiled=True
    ).astype(jnp.float32)
    local_input = arrived_base[0].astype(jnp.float32)
    part_local = arrived_part[0].astype(jnp.float32)
    out_base = (local_input + odd * (part_local + share)).astype(jnp.bfloat16)
    out_part = ((1.0 - odd) * share).astype(jnp.bfloat16)
    local_cotangent = cot_base[0].astype(jnp.float32)
    g_ffn = (odd * local_cotangent + (1.0 - odd) * cot_part[0].astype(jnp.float32)).astype(
        jnp.bfloat16
    )
    g_rows = lax.all_gather(g_ffn, "dp", axis=1, tiled=True)
    g_gathered = g_rows.reshape(tokens, nblk, blk)[:, idx_down].reshape(tokens, hblk, kept * blk)
    down_grad = jnp.einsum(
        "tci,tcm->cim", hidden, g_gathered, preferred_element_type=jnp.float32
    ).astype(jnp.bfloat16)
    g_hidden = jnp.einsum("tcm,cim->tci", g_gathered, w_down, preferred_element_type=jnp.float32)
    sig = jax.nn.sigmoid(pre)
    g_pre = (g_hidden * sig * (1.0 + pre * (1.0 - sig))).astype(jnp.bfloat16)
    up_grad = jnp.einsum(
        "tco,tcm->com", g_pre, gathered, preferred_element_type=jnp.float32
    ).astype(jnp.bfloat16)
    back_terms = jnp.einsum("tco,com->tcm", g_pre, w_up, preferred_element_type=jnp.float32)
    back_partial = place_blocks(back_terms, idx_up, nblk)
    local_scaled_input = local_input / root_mean_square
    local_gain = norm_gain[0].astype(jnp.float32)
    normalized_gradient = lax.psum_scatter(
        back_partial.astype(jnp.bfloat16), "dp", scatter_dimension=1, tiled=True
    ).astype(jnp.float32)
    row_pieces = jnp.sum(
        normalized_gradient * local_gain * local_scaled_input, axis=-1, keepdims=True
    )
    row_statistic = lax.psum(row_pieces, "dp") / width
    centered_gradient = normalized_gradient * local_gain
    base_gradient = (
        (centered_gradient - local_scaled_input * row_statistic) / root_mean_square
        + local_cotangent
    ).astype(jnp.bfloat16)
    g_part = (odd * local_cotangent).astype(jnp.bfloat16)
    gain_gradient = jnp.sum(normalized_gradient * local_scaled_input, axis=0)
    back_base, back_part = passed_along((base_gradient[None], g_part[None]), "pipe", -1)
    return (
        out_base[None],
        out_part[None],
        back_base,
        back_part,
        up_grad[None],
        down_grad[None],
        gain_gradient[None],
    )


def solution(mesh):
    in_specs = (
        P("pipe", None, "dp"),
        P("pipe", None, "dp"),
        P("pipe", None, "dp"),
        P("pipe", None, "dp"),
        P("pipe", "dp"),
        P("pipe", "dp", None, None),
        P("pipe", "dp", None, None),
        P("pipe", "dp", None),
        P("pipe", "dp", None),
    )
    out_specs = (
        P("pipe", None, "dp"),
        P("pipe", None, "dp"),
        P("pipe", None, "dp"),
        P("pipe", None, "dp"),
        P("pipe", "dp", None, None),
        P("pipe", "dp", None, None),
        P("pipe", "dp"),
    )
    return jax.shard_map(
        per_device, mesh=mesh, in_specs=in_specs, out_specs=out_specs, check_vma=False
    )
```

profile of v0, /device:TPU:1, one launch (start us, length us, event | category | flops | bytes accessed | tf_op | source)
XLA Modules:
  0.0 402.2 jit_solution(13859574576922190606)
XLA Ops:
  7.2 1.0 copy.24
  8.3 0.9 copy.25
  9.9 0.9 copy.18
  10.9 4.4 %collective-permute-start = (bf16[1,256,128]{1,2,0:T(8,128)(2,1)S(1)}, bf16[1,256,128]{1,2,0:T(8,128)(2,1)S(1)}, u32[]{:S(2)}, u32[]{:S(2)}) collective-permute-start(bf16[1,256,128]{1,2,0:T(8,128)(2,1)S(1)} %copy.18), channel_id=1, source_target_pairs={{0,32},{32,64},{64,96},{96,128},{128,160},{160,192},{192,224},{224... | collective-permute-start | bytes 196616 | tf_op jit(solution)/shard_map/ppermute | solution.py:11
  15.3 9.2 %collective-permute-done = bf16[1,256,128]{1,2,0:T(8,128)(2,1)S(1)} collective-permute-done((bf16[1,256,128]{1,2,0:T(8,128)(2,1)S(1)}, bf16[1,256,128]{1,2,0:T(8,128)(2,1)S(1)}, u32[]{:S(2)}, u32[]{:S(2)}) %collective-permute-start) | collective-permute-done | bytes 65568 | tf_op jit(solution)/shard_map/ppermute | solution.py:11
  27.5 23.1 %all_gather.10 = bf16[1,4096]{1,0:T(2,128)(2,1)S(1)} all-gather(bf16[1,128]{1,0:T(2,128)(2,1)} %param.13), channel_id=1, replica_groups=mesh['pipe'=16,'dp'=32] {'dp'}, dimensions={1}, use_global_device_ids=true | all-gather | bytes 8448 | tf_op jit(solution)/shard_map/all_gather | solution.py:37
  50.8 25.9 %all-gather.5.cloned.1.call-done = bf16[256,4096]{0,1:T(8,128)(2,1)} async-done(((bf16[256,128]{0,1:T(8,128)(2,1)}), bf16[256,4096]{0,1:T(8,128)(2,1)}) %all-gather.5.cloned.1.call-update) | async-done | bytes 2097168 | tf_op jit(solution)/shard_map/all_gather | solution.py:73
  76.6 4.4 %gather_fusion.1 = bf16[128,256,64]{1,2,0:T(8,128)(2,1)} fusion(bf16[256,64,64]{0,2,1:T(8,128)(2,1)} %bitcast.116, s32[1024]{0:T(1024)S(1)} %pad_clamp_fusion), kind=kCustom, calls=%fused_computation.1 | custom fusion | bytes 8389120 | tf_op jit(solution)/shard_map/gather | solution.py:74
  81.0 57.8 %all-gather.3.cloned.1.call-done = bf16[1,256,4096]{1,2,0:T(8,128)(2,1)} async-done(((bf16[1,256,128]{1,2,0:T(8,128)(2,1)}), bf16[1,256,4096]{1,2,0:T(8,128)(2,1)}) %all-gather.3.cloned.1.call-update) | async-done | bytes 2097168 | tf_op jit(solution)/shard_map/all_gather | solution.py:36
  138.8 2.2 multiply_reduce_fusion
  141.0 1.9 multiply_convert_fusion
  143.0 2.7 gather_fusion
  145.7 3.1 convolution_bitcast_fusion.3
  150.3 4.5 %convolution_bitcast_fusion = f32[256,4,2048]{2,0,1:T(8,128)} fusion(bf16[256,4,64]{0,2,1:T(8,128)(2,1)S(1)} %fusion.12, bf16[1,4,64,2048]{3,2,1,0:T(8,128)(2,1)S(1)} %copy-done), kind=kOutput, calls=%fused_computation.6 | convolution fusion | flops 268435456 | bytes 9568256 | tf_op jit(solution)/shard_map/tco,com->tcm/dot_general | solution.py:84
  154.8 8.7 %copy.27 = f32[256,4,2048]{0,2,1:T(8,128)} copy(f32[256,4,2048]{2,0,1:T(8,128)} %convolution_bitcast_fusion) | data formatting | bytes 16777216 | tf_op jit(solution)/shard_map/tco,com->tcm/transpose | solution.py:84
  163.5 11.1 %convert_bitcast_fusion = bf16[256,64,64]{0,1,2:T(8,128)(2,1)S(1)} fusion(f32[256,128,64]{0,2,1:T(8,128)} %bitcast.114, s32[128]{0:T(128)S(1)} %eq.36), kind=kOutput, calls=%fused_computation.14 | convolution fusion | flops 1611669504 | bytes 10486272 | tf_op jit(solution)/shard_map/tmo,mb->tbo/dot_general | solution.py:19
  174.6 2.6 copy.29
  177.3 4.5 %convolution_bitcast_fusion.1 = f32[256,4,2048]{2,0,1:T(8,128)} fusion(bf16[1,4,64,2048]{3,2,1,0:T(8,128)(2,1)S(1)} %copy-done.2, f32[256,4,64]{0,2,1:T(8,128)S(1)} %convolution_bitcast_fusion.3), kind=kOutput, calls=%fused_computation.7 | convolution fusion | flops 268763136 | bytes 9699328 | tf_op jit(solution)/shard_map/tci,cim->tcm/dot_general | solution.py:60
  181.9 8.7 %copy.21 = f32[256,4,2048]{0,2,1:T(8,128)} copy(f32[256,4,2048]{2,0,1:T(8,128)} %convolution_bitcast_fusion.1) | data formatting | bytes 16777216 | tf_op jit(solution)/shard_map/tci,cim->tcm/transpose | solution.py:60
  190.5 11.2 %convert_bitcast_fusion.1 = bf16[256,64,64]{0,1,2:T(8,128)(2,1)S(1)} fusion(f32[256,128,64]{0,2,1:T(8,128)} %bitcast.115, s32[128]{0:T(128)S(1)} %eq.32), kind=kOutput, calls=%fused_computation.15 | convolution fusion | flops 1611669504 | bytes 10486272 | tf_op jit(solution)/shard_map/tmo,mb->tbo/dot_general | solution.py:19
  201.7 2.5 copy.23
  204.4 3.2 collective-permute-start.1
  207.6 4.4 %collective-permute-start.3 = (bf16[1,256,128]{1,2,0:T(8,128)(2,1)S(1)}, bf16[1,256,128]{1,2,0:T(8,128)(2,1)S(1)}, u32[]{:S(2)}, u32[]{:S(2)}) collective-permute-start(bf16[1,256,128]{1,2,0:T(8,128)(2,1)S(1)} %fusion.28), channel_id=1, source_target_pairs={{0,480},{32,0},{64,32},{96,64},{128,96},{160,128},{192,160},{224,1... | collective-permute-start | bytes 196616 | tf_op jit(solution)/shard_map/ppermute | solution.py:11
  212.1 1.3 collective-permute-done.3
  214.1 4.6 %fusion.5 = bf16[1,4,64,2048]{3,2,1,0:T(8,128)(2,1)} fusion(bf16[256,4,2048]{0,2,1:T(8,128)(2,1)} %bitcast.112, f32[256,4,64]{0,2,1:T(8,128)S(1)} %convolution_bitcast_fusion.3), kind=kOutput, calls=%fused_computation.13 | convolution fusion | flops 269287424 | bytes 5505024 | tf_op jit(solution)/shard_map/tci,tcm->cim/dot_general | solution.py:75
  218.7 57.9 %reduce-scatter.5.cloned.1.call-done = bf16[256,128]{0,1:T(8,128)(2,1)} async-done(((bf16[256,4096]{0,1:T(8,128)(2,1)}), bf16[256,128]{0,1:T(8,128)(2,1)}) %reduce-scatter.5.cloned.1.call-update) | async-done | bytes 65552 | tf_op jit(solution)/shard_map/reduce_scatter | solution.py:88
  276.6 1.5 fusion.25
  278.1 64.3 %psum.7 = f32[256,1]{0,1:T(1,128)S(1)} all-reduce(f32[256,1]{0,1:T(1,128)S(1)} %bitcast.121), channel_id=1, replica_groups=mesh['pipe'=16,'dp'=32] {'dp'}, use_global_device_ids=true, to_apply=%region_4.5 | all-reduce | flops 256 | bytes 2048 | tf_op jit(solution)/shard_map/psum | solution.py:94
  342.3 39.9 %reduce-scatter.3.cloned.1.call-done = bf16[256,128]{0,1:T(8,128)(2,1)} async-done(((bf16[256,4096]{0,1:T(8,128)(2,1)}), bf16[256,128]{0,1:T(8,128)(2,1)}) %reduce-scatter.3.cloned.1.call-update) | async-done | bytes 65552 | tf_op jit(solution)/shard_map/reduce_scatter | solution.py:62
  382.2 1.0 fusion.33
  383.2 5.7 %collective-permute-start.2 = (bf16[1,256,128]{1,2,0:T(8,128)(2,1)S(1)}, bf16[1,256,128]{1,2,0:T(8,128)(2,1)S(1)}, u32[]{:S(2)}, u32[]{:S(2)}) collective-permute-start(bf16[1,256,128]{1,2,0:T(8,128)(2,1)S(1)} %get-tuple-element.16), channel_id=1, source_target_pairs={{0,480},{32,0},{64,32},{96,64},{128,96},{160,128},{192,160},{224,1... | collective-permute-start | bytes 196616 | tf_op jit(solution)/shard_map/ppermute | solution.py:11
  388.9 4.5 %fusion.4 = bf16[1,4,64,2048]{3,2,1,0:T(8,128)(2,1)} fusion(bf16[256,4,64]{0,2,1:T(8,128)(2,1)S(1)} %fusion.12, bf16[256,4,2048]{0,2,1:T(8,128)(2,1)} %bitcast.111), kind=kOutput, calls=%fused_computation.12 | convolution fusion | flops 268959744 | bytes 5373952 | tf_op jit(solution)/shard_map/tco,tcm->com/dot_general | solution.py:81
  (47 shorter events, 8.6 us)
Async XLA Ops:
  7.2 138.6 %copy-start = (bf16[1,4,64,2048]{3,2,1,0:T(8,128)(2,1)S(1)}, bf16[1,4,64,2048]{3,2,1,0:T(8,128)(2,1)}, u32[]{:S(2)}) copy-start(bf16[1,4,64,2048]{3,2,1,0:T(8,128)(2,1)} %param.14) | copy-start | bytes 3145732
  7.2 69.4 %all-gather.5.cloned.1.call-start = ((), (), s32[]{:S(2)}) async-start(), calls=%async_computation.4 | async-start | bytes 2162688 | tf_op jit(solution)/shard_map/all_gather | solution.py:73
  9.9 129.0 %all-gather.3.cloned.1.call-start = ((), (), s32[]{:S(2)}) async-start(), calls=%async_computation.2 | async-start | bytes 2162688 | tf_op jit(solution)/shard_map/all_gather | solution.py:36
  10.9 13.6 %collective-permute-start = (bf16[1,256,128]{1,2,0:T(8,128)(2,1)S(1)}, bf16[1,256,128]{1,2,0:T(8,128)(2,1)S(1)}, u32[]{:S(2)}, u32[]{:S(2)}) collective-permute-start(bf16[1,256,128]{1,2,0:T(8,128)(2,1)S(1)} %copy.18), channel_id=1, source_target_pairs={{0,32},{32,64},{64,96},{96,128},{128,160},{160,192},{192,224},{224... | collective-permute-start | bytes 196616 | tf_op jit(solution)/shard_map/ppermute | solution.py:11
  24.5 0.6 copy-start.3
  25.1 251.4 %reduce-scatter.5.cloned.1.call-start = ((), (), s32[]{:S(2)}) async-start(), calls=%async_computation.5 | async-start | bytes 2162688 | tf_op jit(solution)/shard_map/reduce_scatter | solution.py:88
  145.7 3.4 copy-start.1
  145.7 3.7 copy-start.2
  174.6 2.6 copy-start.6
  177.2 205.0 %reduce-scatter.3.cloned.1.call-start = ((), (), s32[]{:S(2)}) async-start(), calls=%async_computation.3 | async-start | bytes 2162688 | tf_op jit(solution)/shard_map/reduce_scatter | solution.py:62
  201.7 2.6 copy-start.5
  201.7 10.3 %copy-start.7 = (bf16[1,128]{1,0:T(2,128)(2,1)S(1)}, bf16[1,128]{1,0:T(2,128)(2,1)}, u32[]{:S(2)}) copy-start(bf16[1,128]{1,0:T(2,128)(2,1)} %param.13) | copy-start | bytes 772
  204.2 72.3 %copy-start.4 = (bf16[1,256,128]{1,2,0:T(8,128)(2,1)S(1)}, bf16[1,256,128]{1,2,0:T(8,128)(2,1)}, u32[]{:S(2)}) copy-start(bf16[1,256,128]{1,2,0:T(8,128)(2,1)} %copy-done.3) | copy-start | bytes 196612
  204.4 137.9 %collective-permute-start.1 = (bf16[1,256,128]{1,2,0:T(8,128)(2,1)S(1)}, bf16[1,256,128]{1,2,0:T(8,128)(2,1)S(1)}, u32[]{:S(2)}, u32[]{:S(2)}) collective-permute-start(bf16[1,256,128]{1,2,0:T(8,128)(2,1)S(1)} %copy.19), channel_id=1, source_target_pairs={{0,32},{32,64},{64,96},{96,128},{128,160},{160,192},{192,224},{224... | collective-permute-start | bytes 196616 | tf_op jit(solution)/shard_map/ppermute | solution.py:11
  207.6 5.7 %collective-permute-start.3 = (bf16[1,256,128]{1,2,0:T(8,128)(2,1)S(1)}, bf16[1,256,128]{1,2,0:T(8,128)(2,1)S(1)}, u32[]{:S(2)}, u32[]{:S(2)}) collective-permute-start(bf16[1,256,128]{1,2,0:T(8,128)(2,1)S(1)} %fusion.28), channel_id=1, source_target_pairs={{0,480},{32,0},{64,32},{96,64},{128,96},{160,128},{192,160},{224,1... | collective-permute-start | bytes 196616 | tf_op jit(solution)/shard_map/ppermute | solution.py:11
  383.2 11.7 %collective-permute-start.2 = (bf16[1,256,128]{1,2,0:T(8,128)(2,1)S(1)}, bf16[1,256,128]{1,2,0:T(8,128)(2,1)S(1)}, u32[]{:S(2)}, u32[]{:S(2)}) collective-permute-start(bf16[1,256,128]{1,2,0:T(8,128)(2,1)S(1)} %get-tuple-element.16), channel_id=1, source_target_pairs={{0,480},{32,0},{64,32},{96,64},{128,96},{160,128},{192,160},{224,1... | collective-permute-start | bytes 196616 | tf_op jit(solution)/shard_map/ppermute | solution.py:11
Sparse Core Ops, SparseCore 0:
  11.7 64.8 all-gather.4
  80.3 58.4 all-gather.2
  177.3 99.2 reduce-scatter.4
  280.8 101.3 reduce-scatter.2
where the time goes:
time: 404 us; the launch traced here: 402 us
  waiting for transfers between devices  192 us (48%)
  blocking collectives  87.4 us (22%)
  matrix products  44.4 us (11%)
  local copies, waits for them, and re-layouts  37.8 us (9%)
  starting transfers between devices  17.8 us (4%)
  between operations  14 us (3%)
  other arithmetic  8.68 us (2%)
    psum x1, blocking collectives, per_device(): row_statistic = lax.psum(row_pieces, 'dp') / width  64.3 us
    reduce_scatter x1, waiting for transfers between devices, per_device(): lax.psum_scatter(back_partial.astype(jnp.bfloat16), 'dp', scatter_dimensi...  57.9 us
    all_gather x1, waiting for transfers between devices, per_device(): lax.all_gather(arrived_base, 'dp', axis=2, tiled=True)  57.8 us
    reduce_scatter x1, waiting for transfers between devices, per_device(): lax.psum_scatter(partial_value.astype(jnp.bfloat16), 'dp', scatter_dimens...  39.9 us
    all_gather x1, waiting for transfers between devices, per_device(): g_rows = lax.all_gather(g_ffn, 'dp', axis=1, tiled=True)  25.9 us
    all_gather x1, blocking collectives, per_device(): lax.all_gather(norm_gain, 'dp', axis=1, tiled=True)  23.1 us
    dot_general x2, matrix products, place_blocks(): jnp.einsum('tmo,mb->tbo', pieces, onehot, precision=lax.Precision.HIGHEST)  22.3 us
    ppermute x4, starting transfers between devices, passed_along(): lax.ppermute(shard, axis, [(i, (i + by) % count) for i in range(count)])  17.7 us
  transfers between devices with their start and end apart: 8, of which 6 were waited for; matrix products, arithmetic and copies ran while one was open for 12% of the time, Pallas kernels for 0%

commit v1 on v0

v1 whole, which is shorter than its diff:
```python
import functools

import jax
import jax.numpy as jnp
from jax import lax
from jax.experimental import pallas as pl
from jax.experimental.pallas import tpu as pltpu
from jax.sharding import PartitionSpec as P

eps = 1e-05
LANES = 128
EXTRA = 16
F32 = jnp.float32
BF16 = jnp.bfloat16
VMEM = pl.BlockSpec(memory_space=pltpu.VMEM)
SMEM = pl.BlockSpec(memory_space=pltpu.SMEM)
HBM = pl.BlockSpec(memory_space=pltpu.HBM)
PARAMS = pltpu.CompilerParams(vmem_limit_bytes=40 * 1024 * 1024)


def passed_along(shard, axis, by):
    count = lax.axis_size(axis)
    return lax.ppermute(shard, axis, [(i, (i + by) % count) for i in range(count)])


def other_core(shard):
    count = lax.axis_size("dp")
    return lax.ppermute(shard, "dp", [(i, i ^ 1) for i in range(count)])


def after(value, earlier):
    return lax.optimization_barrier((value, earlier))[0]


def exchange(chunks):
    return lax.all_to_all(chunks, "dp", 0, 0, tiled=True)


def pack_kernel(odd_ref, base_ref, cot_base_ref, cot_part_ref, gain_ref, out_ref):
    count, rows, _ = out_ref.shape
    half = base_ref.shape[0] // 2
    odd = odd_ref[0] == 1
    gain = jnp.broadcast_to(gain_ref[...].astype(F32), (EXTRA, LANES)).astype(BF16)
    for j in range(count):
        at = pl.ds((j % 2) * half, half)
        out_ref[j, :half, :] = base_ref[at, :]
        out_ref[j, half : 2 * half, :] = jnp.where(odd, cot_base_ref[at, :], cot_part_ref[at, :])
        out_ref[j, 2 * half :, :] = gain


def pack(odd, base, cot_base, cot_part, gain, count):
    return pl.pallas_call(
        pack_kernel,
        out_shape=jax.ShapeDtypeStruct((count, base.shape[0] + EXTRA, LANES), BF16),
        in_specs=[SMEM, VMEM, VMEM, VMEM, VMEM],
        out_specs=VMEM,
        compiler_params=PARAMS,
        cost_estimate=pl.CostEstimate(flops=1_000_000, bytes_accessed=2_500_000, transcendentals=0),
        name="pack_chunks",
    )(odd[None], base, cot_base, cot_part, gain)


def merge_tiles(tile0, tile1, turned0, turned1, kept0, kept1, lower):
    low = jnp.where(lower, 1.0, 0.0).astype(BF16)
    high = jnp.where(lower, 0.0, 1.0).astype(BF16)
    swapped = tile1 * low + tile0 * high
    swapped = jnp.concatenate([swapped[:, 64:], swapped[:, :64]], axis=1)
    first = jnp.where(lower, kept0 * (1 - turned0), 0).astype(F32).astype(BF16)
    second = jnp.where(lower, 0, kept1 * (1 - turned1)).astype(F32).astype(BF16)
    third = jnp.where(lower, kept0 * turned0, kept1 * turned1).astype(F32).astype(BF16)
    return tile0 * first + tile1 * second + swapped * third


def tile_at(n):
    return pl.ds(pl.multiple_of(n * LANES, LANES), LANES)


def densify_kernel(idx_up, idx_down, up_ref, down_ref, out_ref, dense, sems):
    hblk, blk, wide = up_ref.shape
    kept = idx_up.shape[1]
    tiles = out_ref.shape[1] // LANES
    units = hblk * blk
    lower = lax.broadcasted_iota(jnp.int32, (1, LANES), 1) < blk
    copies = []
    for which, (idx, src) in enumerate(((idx_up, up_ref), (idx_down, down_ref))):

        def step(j, ats, which=which, idx=idx, src=src):
            plans, next_ats = [], []
            for c in range(hblk):
                p0 = jnp.minimum(ats[c], kept - 1)
                m0 = jnp.where((ats[c] < kept) & (idx[c, p0] == 2 * j), 1, 0)
                middle = ats[c] + m0
                p1 = jnp.minimum(middle, kept - 1)
                m1 = jnp.where((middle < kept) & (idx[c, p1] == 2 * j + 1), 1, 0)
                plans.append((p0, m0, p1, m1))
                next_ats.append(middle + m1)
            loaded = [
                (src[c, :, tile_at(p0 // 2)], src[c, :, tile_at(p1 // 2)])
                for c, (p0, m0, p1, m1) in enumerate(plans)
            ]
            merged = [
                merge_tiles(tile0, tile1, p0 % 2, 1 - p1 % 2, m0, m1, lower)
                for (tile0, tile1), (p0, m0, p1, m1) in zip(loaded, plans)
            ]
            for c in range(hblk):
                dense[pl.ds(which * units + c * blk, blk), tile_at(j)] = merged[c]
            return tuple(next_ats)

        lax.fori_loop(0, tiles, step, (jnp.int32(0),) * hblk, unroll=2)
        rows = pl.ds(which * units, units)
        copies.append(pltpu.make_async_copy(dense.at[rows], out_ref.at[rows], sems.at[which]))
        copies[-1].start()
    for copy in copies:
        copy.wait()


def densify(idx_up, idx_down, up, down, width):
    hblk, blk, _ = up.shape
    return pl.pallas_call(
        densify_kernel,
        out_shape=jax.ShapeDtypeStruct((2 * hblk * blk, width), BF16),
        in_specs=[SMEM, SMEM, VMEM, VMEM],
        out_specs=HBM,
        scratch_shapes=[pltpu.VMEM((2 * hblk * blk, width), BF16), pltpu.SemaphoreType.DMA((2,))],
        compiler_params=PARAMS,
        cost_estimate=pl.CostEstimate(flops=10_000_000, bytes_accessed=6_291_456, transcendentals=0),
        name="densify",
    )(idx_up, idx_down, up, down)


def dot_nt(a, b):
    return lax.dot_general(a, b, (((1,), (1,)), ((), ())), preferred_element_type=F32)


def dot_nn(a, b):
    return lax.dot_general(a, b, (((1,), (0,)), ((), ())), preferred_element_type=F32)


def split3(value):
    high = value.astype(BF16).astype(F32)
    rest = value - high
    middle = rest.astype(BF16).astype(F32)
    return high, middle, rest - middle


def main_kernel(
    rows_ref, own_hbm, other_hbm, back_hbm, swap_ref, keep_ref, weights, back_ref, in_sems, out_sems
):
    count = rows_ref.shape[0]
    tokens = (rows_ref.shape[1] - EXTRA) // 2
    width = count * LANES
    units = own_hbm.shape[0] // 2
    loads = []
    for n, (source, which) in enumerate(((own_hbm, 0), (other_hbm, 0), (own_hbm, 1), (other_hbm, 1))):
        loads.append(
            pltpu.make_async_copy(
                source.at[pl.ds(which * units, units)], weights.at[n], in_sems.at[n]
            )
        )
        loads[-1].start()
    squares = jnp.zeros((tokens, LANES), F32)
    for j in range(count):
        x = rows_ref[j, :tokens, :].astype(F32)
        squares = squares + x * x
    mean_square = jnp.sum(squares, axis=-1, keepdims=True) / width
    inverse = 1.0 / jnp.sqrt(mean_square + eps)
    for j in range(count):
        x = rows_ref[j, :tokens, :].astype(F32)
        gain = rows_ref[j, 2 * tokens :, :].astype(F32)[:1]
        swap_ref[j] = (x * inverse * gain).astype(BF16)
        swap_ref[count + j] = rows_ref[j, tokens : 2 * tokens, :]
    normed = jnp.concatenate([swap_ref[j] for j in range(count)], axis=1)
    g_rows = jnp.concatenate(
        [rows_ref[j, tokens : 2 * tokens, :] for j in range(count)], axis=1
    )
    pres, g_hiddens = [], []
    for n in range(2):
        loads[n].wait()
        pres.append(dot_nt(normed, weights[n]))
    for n in range(2):
        loads[2 + n].wait()
        g_hiddens.append(dot_nt(g_rows, weights[2 + n]))
    per = units // LANES
    stat = jnp.zeros((tokens, 1), F32)
    hiddens, g_pres = [], []
    for n, (pre, g_hidden) in enumerate(zip(pres, g_hiddens)):
        sig = 1.0 / (1.0 + jnp.exp(-pre))
        hidden = (pre * sig).astype(BF16)
        g_pre = (g_hidden * sig * (1.0 + pre * (1.0 - sig))).astype(BF16)
        stat = stat + jnp.sum(g_pre.astype(F32) * pre, axis=-1, keepdims=True)
        for k in range(per):
            at = slice(k * LANES, (k + 1) * LANES)
            if n == 0:
                keep_ref[k] = hidden[:, at]
                keep_ref[per + k] = g_pre[:, at]
            else:
                swap_ref[2 * count + k] = hidden[:, at]
                swap_ref[2 * count + per + k] = g_pre[:, at]
        hiddens.append(hidden)
        g_pres.append(g_pre)
    stat_high, stat_low, _ = split3(stat)
    lane = lax.broadcasted_iota(jnp.int32, (tokens, LANES), 1)
    columns = jnp.zeros((tokens, LANES), F32)
    for k, part in enumerate((stat_high, stat_low) + split3(inverse)):
        columns = jnp.where(lane == k, part, columns)
    riding = jnp.transpose(columns)[:EXTRA].astype(BF16)
    step = 1024
    stores = []
    for n, s in enumerate(range(0, width, step)):
        back = dot_nn(g_pres[0], weights[0, :, s : s + step]) + dot_nn(
            g_pres[1], weights[1, :, s : s + step]
        )
        ffn = dot_nn(hiddens[0], weights[2, :, s : s + step]) + dot_nn(
            hiddens[1], weights[3, :, s : s + step]
        )
        for k in range(step // LANES):
            j = s // LANES + k
            at = slice(k * LANES, (k + 1) * LANES)
            back_ref[j, :tokens, :] = back[:, at].astype(BF16)
            back_ref[j, tokens : 2 * tokens, :] = ffn[:, at].astype(BF16)
            back_ref[j, 2 * tokens :, :] = riding
        at = pl.ds(s // LANES, step // LANES)
        stores.append(pltpu.make_async_copy(back_ref.at[at], back_hbm.at[at], out_sems.at[n]))
        stores[-1].start()
    for store in stores:
        store.wait()


def main(rows, own, other):
    count = rows.shape[0]
    tokens = (rows.shape[1] - EXTRA) // 2
    units, width = own.shape[0] // 2, own.shape[1]
    per = units // LANES
    return pl.pallas_call(
        main_kernel,
        out_shape=(
            jax.ShapeDtypeStruct(rows.shape, BF16),
            jax.ShapeDtypeStruct((2 * count + 2 * per, tokens, LANES), BF16),
            jax.ShapeDtypeStruct((2 * per, tokens, LANES), BF16),
        ),
        in_specs=[VMEM, HBM, HBM],
        out_specs=[HBM, VMEM, VMEM],
        scratch_shapes=[
            pltpu.VMEM((4, units, width), BF16),
            pltpu.VMEM(rows.shape, BF16),
            pltpu.SemaphoreType.DMA((4,)),
            pltpu.SemaphoreType.DMA((width // 1024,)),
        ],
        compiler_params=PARAMS,
        cost_estimate=pl.CostEstimate(flops=2_200_000_000, bytes_accessed=16_000_000, transcendentals=65_536),
        name="forward_backward",
    )(rows, own, other)


def grads_kernel(idx_up, idx_down, mine_ref, keep_ref, theirs_ref, up_ref, down_ref, dense):
    hblk, blk, wide = up_ref.shape
    per = hblk * blk // LANES
    count = (mine_ref.shape[0] - 2 * per) // 2
    lower = lax.broadcasted_iota(jnp.int32, (1, LANES), 1) < blk
    group = 8

    def left(n):
        tiles = [
            jnp.concatenate([keep_ref[n * per + k], theirs_ref[2 * count + n * per + k]], axis=0)
            for k in range(per)
        ]
        return jnp.concatenate(tiles, axis=1)

    for n, first, idx, out in ((0, count, idx_down, down_ref), (1, 0, idx_up, up_ref)):
        turned = jnp.transpose(left(n))
        for s in range(0, count, group):
            rows = jnp.concatenate(
                [
                    jnp.concatenate([mine_ref[first + j], theirs_ref[first + j]], axis=0)
                    for j in range(s, s + group)
                ],
                axis=1,
            )
            dense[:, s * LANES : (s + group) * LANES] = dot_nn(turned, rows).astype(BF16)
        def step(j, carry, idx=idx, out=out):
            merged = []
            for c in range(hblk):
                e0, e1 = idx[c, 2 * j], idx[c, 2 * j + 1]
                rows = pl.ds(c * blk, blk)
                merged.append(
                    merge_tiles(
                        dense[rows, tile_at(e0 // 2)],
                        dense[rows, tile_at(e1 // 2)],
                        e0 % 2,
                        1 - e1 % 2,
                        1,
                        1,
                        lower,
                    )
                )
            for c in range(hblk):
                out[c, :, tile_at(j)] = merged[c]
            return carry

        lax.fori_loop(0, wide // LANES, step, 0, unroll=2)


def grads(idx_up, idx_down, mine, keep, theirs, shape, width):
    hblk, blk, _ = shape
    return pl.pallas_call(
        grads_kernel,
        out_shape=(jax.ShapeDtypeStruct(shape, BF16), jax.ShapeDtypeStruct(shape, BF16)),
        in_specs=[SMEM, SMEM, VMEM, VMEM, VMEM],
        out_specs=[VMEM, VMEM],
        scratch_shapes=[pltpu.VMEM((hblk * blk, width), BF16)],
        compiler_params=PARAMS,
        cost_estimate=pl.CostEstimate(flops=1_000_000, bytes_accessed=100_000, transcendentals=0),
        name="weight_gradients",
    )(idx_up, idx_down, mine, keep, theirs)


def finish_kernel(width, parts_ref, base_ref, gain_ref, cot_ref, out_ref, gain_out_ref):
    count = parts_ref.shape[0]
    tokens = (parts_ref.shape[1] - EXTRA) // 2
    gain = gain_ref[...].astype(F32)
    total_gain = jnp.zeros((1, LANES), F32)
    for half in range(2):
        total = jnp.zeros((tokens, LANES), F32)
        riding = jnp.zeros((EXTRA, LANES), F32)
        for j in range(half, count, 2):
            total = total + parts_ref[j, :tokens, :].astype(F32)
            riding = riding + parts_ref[j, 2 * tokens :, :].astype(F32)
        first = parts_ref[half, 2 * tokens :, :].astype(F32)
        summed = (riding[0:1] + riding[1:2]) / width
        inverse = first[2:3] + first[3:4] + first[4:5]
        row = lax.broadcasted_iota(jnp.int32, (LANES, LANES), 0)
        turned = jnp.transpose(jnp.where(row == 0, summed, jnp.where(row == 1, inverse, 0.0)))
        stat = turned[:, 0:1]
        inverse = turned[:, 1:2]
        at = pl.ds(half * tokens, tokens)
        scaled = base_ref[at, :].astype(F32) * inverse
        out_ref[at, :] = (
            (total * gain - scaled * stat) * inverse + cot_ref[at, :].astype(F32)
        ).astype(BF16)
        total_gain = total_gain + jnp.sum(total * scaled, axis=0, keepdims=True)
    gain_out_ref[...] = total_gain


def finish(parts, base, gain, cot, width):
    return pl.pallas_call(
        functools.partial(finish_kernel, width),
        out_shape=(
            jax.ShapeDtypeStruct(base.shape, BF16),
            jax.ShapeDtypeStruct((1, LANES), F32),
        ),
        in_specs=[VMEM] * 4,
        out_specs=[VMEM] * 2,
        compiler_params=PARAMS,
        cost_estimate=pl.CostEstimate(flops=2_000_000, bytes_accessed=1_500_000, transcendentals=0),
        name="input_gradient",
    )(parts, base, gain, cot)


def outputs_kernel(odd_ref, parts_ref, base_ref, part_ref, out_base_ref, out_part_ref):
    count = parts_ref.shape[0]
    tokens = (parts_ref.shape[1] - EXTRA) // 2
    odd = odd_ref[0].astype(F32)
    for half in range(2):
        total = jnp.zeros((tokens, LANES), F32)
        for j in range(half, count, 2):
            total = total + parts_ref[j, tokens : 2 * tokens, :].astype(F32)
        at = pl.ds(half * tokens, tokens)
        part = part_ref[at, :].astype(F32)
        out_base_ref[at, :] = (base_ref[at, :].astype(F32) + odd * (part + total)).astype(BF16)
        out_part_ref[at, :] = ((1.0 - odd) * total).astype(BF16)


def outputs(odd, parts, base, part):
    return pl.pallas_call(
        outputs_kernel,
        out_shape=(jax.ShapeDtypeStruct(base.shape, BF16), jax.ShapeDtypeStruct(base.shape, BF16)),
        in_specs=[SMEM, VMEM, VMEM, VMEM],
        out_specs=[VMEM] * 2,
        compiler_params=PARAMS,
        cost_estimate=pl.CostEstimate(flops=2_000_000, bytes_accessed=1_500_000, transcendentals=0),
        name="section_outputs",
    )(odd[None], parts, base, part)


def per_device(
    sent_base,
    sent_part,
    cot_base,
    cot_part,
    norm_gain,
    up_blocks,
    down_blocks,
    up_index,
    down_index,
):
    count = lax.axis_size("dp")
    tokens, lanes = sent_base.shape[1:]
    width = count * lanes
    odd = lax.axis_index("pipe") % 2

    arrived_base = passed_along(sent_base[0], "pipe", 1)
    own = densify(up_index[0], down_index[0], up_blocks[0], down_blocks[0], width)
    packed = pack(odd, after(arrived_base, own), cot_base[0], cot_part[0], norm_gain, count)
    rows = exchange(packed)
    other = other_core(after(own, packed))
    g_part = jnp.where(odd == 1, cot_base[0], jnp.zeros_like(cot_base[0]))
    back_part = passed_along(after(g_part, packed), "pipe", -1)
    arrived_part = passed_along(after(sent_part[0], packed), "pipe", 1)
    own_later, back_part, arrived_part = lax.optimization_barrier((own, back_part, arrived_part))

    parts, swap, keep = main(rows, own_later, other)
    theirs = other_core(swap)
    up_grad, down_grad = grads(
        up_index[0], down_index[0], swap, keep, theirs, up_blocks.shape[1:], width
    )
    part_rows = exchange(parts)
    up_grad, down_grad, part_rows = lax.optimization_barrier((up_grad, down_grad, part_rows))
    base_gradient, gain_gradient = finish(part_rows, arrived_base, norm_gain, cot_base[0], width)
    back_base = passed_along(base_gradient, "pipe", -1)
    out_base, out_part = outputs(odd, part_rows, arrived_base, arrived_part)
    return (
        out_base[None],
        out_part[None],
        back_base[None],
        back_part[None],
        up_grad[None],
        down_grad[None],
        gain_gradient,
    )


def solution(mesh):
    in_specs = (
        P("pipe", None, "dp"),
        P("pipe", None, "dp"),
        P("pipe", None, "dp"),
        P("pipe", None, "dp"),
        P("pipe", "dp"),
        P("pipe", "dp", None, None),
        P("pipe", "dp", None, None),
        P("pipe", "dp", None),
        P("pipe", "dp", None),
    )
    out_specs = (
        P("pipe", None, "dp"),
        P("pipe", None, "dp"),
        P("pipe", None, "dp"),
        P("pipe", None, "dp"),
        P("pipe", "dp", None, None),
        P("pipe", "dp", None, None),
        P("pipe", "dp"),
    )
    return jax.shard_map(
        per_device, mesh=mesh, in_specs=in_specs, out_specs=out_specs, check_vma=False
    )
```

time: 404 us -> 121 us (0.30)
  waiting for transfers between devices: 192 us -> 40.7 us
  blocking collectives: 87.4 us -> 0 us
  matrix products: 44.4 us -> 0 us
  local copies, waits for them, and re-layouts: 37.8 us -> 7.89 us
  Pallas kernels: 0 us -> 29.3 us
  starting transfers between devices: 17.8 us -> 41.5 us
  between operations: 14 us -> 0.84 us
  other arithmetic: 8.68 us -> 0.01 us
    reduce_scatter x2 -> x0, waiting for transfers between devices: 97.8 us -> none  [the longest x1 57.9 us: per_device(): lax.psum_scatter(back_partial.astype(jnp.bfloat16), 'dp', scatter_dimensi...]
    all_gather x2 -> x0, waiting for transfers between devices: 83.7 us -> none  [the longest x1 57.8 us: per_device(): lax.all_gather(arrived_base, 'dp', axis=2, tiled=True)]
    psum x1 -> x0, blocking collectives: 64.3 us -> none  [per_device(): row_statistic = lax.psum(row_pieces, 'dp') / width]
    dot_general x8 -> x0, matrix products: 44.4 us -> none  [the longest x2 22.3 us: place_blocks(): jnp.einsum('tmo,mb->tbo', pieces, onehot, precision=lax.Precision.HIGHEST)]
    all_to_all x0 -> x2, waiting for transfers between devices: none -> 35.2 us  [exchange(): return lax.all_to_all(chunks, 'dp', 0, 0, tiled=True)]
    pallas_call x0 -> x6, Pallas kernels: none -> 29.3 us  [the longest x1 10.3 us: main(): pl.pallas_call(main_kernel, out_shape=(jax.ShapeDtypeStruct(rows.shape, B...]
    all_gather x1 -> x0, blocking collectives: 23.1 us -> none  [per_device(): lax.all_gather(norm_gain, 'dp', axis=1, tiled=True)]
    transpose x2 -> x0, local copies, waits for them, and re-layouts: 17.3 us -> none  [the longest x1 8.67 us: per_device(): jnp.einsum('tco,com->tcm', g_pre, w_up, preferred_element_type=jnp.float32)]
  transfers between devices with their start and end apart: 8 -> 8, of which waited for: 6 -> 5; matrix products, arithmetic and copies ran while one was open for 12% -> 0% of each run, Pallas kernels for 0% -> 15%
where the time goes in v1:
time: 121 us; the launch traced here: 120 us
  starting transfers between devices  41.5 us (34%)
  waiting for transfers between devices  40.7 us (34%)
  Pallas kernels  29.3 us (24%)
  local copies, waits for them, and re-layouts  7.89 us (7%)
    all_to_all x2, waiting for transfers between devices, exchange(): return lax.all_to_all(chunks, 'dp', 0, 0, tiled=True)  35.2 us
    ppermute x4, starting transfers between devices, passed_along(): lax.ppermute(shard, axis, [(i, (i + by) % count) for i in range(count)])  24.5 us
    pallas_call x1, Pallas kernels, main(): pl.pallas_call(main_kernel, out_shape=(jax.ShapeDtypeStruct(rows.shape, B...  10.3 us
    ppermute x2, starting transfers between devices, other_core(): return lax.ppermute(shard, 'dp', [(i, i ^ 1) for i in range(count)])  9.26 us
    pallas_call x1, Pallas kernels, densify(): pl.pallas_call(densify_kernel, out_shape=jax.ShapeDtypeStruct((2 * hblk *...  9.05 us
    pallas_call x1, Pallas kernels, grads(): pl.pallas_call(grads_kernel, out_shape=(jax.ShapeDtypeStruct(shape, BF16)...  8.08 us
    unnamed x26, local copies, waits for them, and re-layouts  7.89 us
    all_to_all x2, starting transfers between devices, exchange(): return lax.all_to_all(chunks, 'dp', 0, 0, tiled=True)  7.71 us
  transfers between devices with their start and end apart: 8, of which 5 were waited for; matrix products, arithmetic and copies ran while one was open for 0% of the time, Pallas kernels for 15%

profile of v1, /device:TPU:1, one launch (start us, length us, event | category | flops | bytes accessed | tf_op | source)
XLA Modules:
  0.0 120.2 jit_solution(5221727550892461211)
XLA Ops:
  0.6 4.4 %collective-permute-start = (bf16[256,128]{1,0:T(8,128)(2,1)}, bf16[256,128]{1,0:T(8,128)(2,1)S(1)}, u32[]{:S(2)}, u32[]{:S(2)}) collective-permute-start(bf16[256,128]{1,0:T(8,128)(2,1)} %bitcast.29), channel_id=1, source_target_pairs={{0,32},{32,64},{64,96},{96,128},{128,160},{160,192},{192,224},{224... | collective-permute-start | bytes 196616 | tf_op jit(solution)/shard_map/ppermute | solution.py:23
  5.0 1.2 %copy-done.2 = bf16[1,4,64,2048]{3,2,1,0:T(8,128)(2,1)S(1)} copy-done((bf16[1,4,64,2048]{3,2,1,0:T(8,128)(2,1)S(1)}, bf16[1,4,64,2048]{3,2,1,0:T(8,128)(2,1)}, u32[]{:S(2)}) %copy-start.2) | copy-done | bytes 1048600
  6.3 1.2 %copy-done.3 = bf16[1,4,64,2048]{3,2,1,0:T(8,128)(2,1)S(1)} copy-done((bf16[1,4,64,2048]{3,2,1,0:T(8,128)(2,1)S(1)}, bf16[1,4,64,2048]{3,2,1,0:T(8,128)(2,1)}, u32[]{:S(2)}) %copy-start.3) | copy-done | bytes 1048600
  7.5 0.7 copy-done.6
  8.2 0.7 copy-done.8
  8.8 9.1 %densify.1.own_hbm = bf16[512,4096]{1,0:T(8,128)(2,1)} custom-call(s32[4,32]{1,0:T(4,128)S(1)} %bitcast.21, s32[4,32]{1,0:T(4,128)S(1)} %bitcast.23, bf16[4,64,2048]{2,1,0:T(8,128)(2,1)S(1)} %bitcast.16, bf16[4,64,2048]{2,1,0:T(8,128)(2,1)S(1)} %bitcast.17), custom_call_target="tpu_custom_call" | custom-call | flops 10000000 | bytes 6291456 | tf_op jit(solution)/shard_map/densify/pallas_call | solution.py:119
  17.9 0.0 collective-permute-done.base_ref
  17.9 0.3 pack_chunks.1
  18.2 1.4 %copy-done = bf16[32,272,128]{2,1,0:T(8,128)(2,1)} copy-done((bf16[32,272,128]{2,1,0:T(8,128)(2,1)}, bf16[32,272,128]{2,1,0:T(8,128)(2,1)S(1)}, u32[]{:S(2)}) %copy-start) | copy-done | bytes 2228248
  19.7 6.5 %collective-permute-start.3 = (bf16[512,4096]{1,0:T(8,128)(2,1)}, bf16[512,4096]{1,0:T(8,128)(2,1)}, u32[]{:S(2)}, u32[]{:S(2)}) collective-permute-start(bf16[512,4096]{1,0:T(8,128)(2,1)} %densify.1.own_hbm), channel_id=1, source_target_pairs={{0,1},{1,0},{2,3},{3,2},{4,5},{5,4},{6,7},{7,6},{8,9},{9,8},{10,11... | collective-permute-start | bytes 12582920 | tf_op jit(solution)/shard_map/ppermute | solution.py:28
  26.1 3.9 %all-to-all-start = ((bf16[32,272,128]{2,1,0:T(8,128)(2,1)}), bf16[32,272,128]{2,1,0:T(8,128)(2,1)S(1)}, u32[]{:S(2)}, u32[]{:S(2)}) async-start(bf16[32,272,128]{2,1,0:T(8,128)(2,1)} %copy-done), calls=%async_computation | async-start | bytes 4456448 | tf_op jit(solution)/shard_map/all_to_all | solution.py:36
  30.0 9.1 %collective-permute-start.1 = (bf16[256,128]{1,0:T(8,128)(2,1)S(1)}, bf16[256,128]{1,0:T(8,128)(2,1)S(1)}, u32[]{:S(2)}, u32[]{:S(2)}) collective-permute-start(bf16[256,128]{1,0:T(8,128)(2,1)S(1)} %broadcast_select_fusion), channel_id=1, source_target_pairs={{0,480},{32,0},{64,32},{96,64},{128,96},{160,128},{192,160},{224,1... | collective-permute-start | bytes 196616 | tf_op jit(solution)/shard_map/ppermute | solution.py:23
  39.1 1.9 %collective-permute-start.2 = (bf16[256,128]{1,0:T(8,128)(2,1)S(1)}, bf16[256,128]{1,0:T(8,128)(2,1)S(1)}, u32[]{:S(2)}, u32[]{:S(2)}) collective-permute-start(bf16[256,128]{1,0:T(8,128)(2,1)S(1)} %bitcast.30), channel_id=1, source_target_pairs={{0,32},{32,64},{64,96},{96,128},{128,160},{160,192},{192,224},{224... | collective-permute-start | bytes 196616 | tf_op jit(solution)/shard_map/ppermute | solution.py:23
  41.1 0.0 collective-permute-done.1
  41.1 4.6 %collective-permute-done.2.part_ref = bf16[256,128]{1,0:T(8,128)(2,1)S(1)} collective-permute-done((bf16[256,128]{1,0:T(8,128)(2,1)S(1)}, bf16[256,128]{1,0:T(8,128)(2,1)S(1)}, u32[]{:S(2)}, u32[]{:S(2)}) %collective-permute-start.2) | collective-permute-done | bytes 65568 | tf_op jit(solution)/shard_map/ppermute | solution.py:23
  45.6 14.0 %all-to-all-done.rows_ref = bf16[32,272,128]{2,1,0:T(8,128)(2,1)S(1)} async-done(((bf16[32,272,128]{2,1,0:T(8,128)(2,1)}), bf16[32,272,128]{2,1,0:T(8,128)(2,1)S(1)}, u32[]{:S(2)}, u32[]{:S(2)}) %all-to-all-start) | async-done | bytes 2228256 | tf_op jit(solution)/shard_map/all_to_all | solution.py:36
  59.6 0.0 collective-permute-done.3.other_hbm
  59.7 10.3 %forward_backward.1 = (bf16[32,272,128]{2,1,0:T(8,128)(2,1)S(1)}, bf16[68,128,128]{2,1,0:T(8,128)(2,1)}, bf16[4,128,128]{2,1,0:T(8,128)(2,1)S(1)}) custom-call(bf16[32,272,128]{2,1,0:T(8,128)(2,1)S(1)} %all-to-all-done.rows_ref, bf16[512,4096]{1,0:T(8,128)(2,1)} %densify.1.own_hbm, bf16[512,4096]{1,0:T(8,128)(2,1)} %collective-permute-done.3.other_hbm), custom_call_target="tpu_custom_call" | custom-call | flops 2200000000 | bytes 16000000 | tf_op jit(solution)/shard_map/forward_backward/pallas_call | solution.py:234
  69.9 1.4 %copy-done.1 = bf16[32,272,128]{2,1,0:T(8,128)(2,1)} copy-done((bf16[32,272,128]{2,1,0:T(8,128)(2,1)}, bf16[32,272,128]{2,1,0:T(8,128)(2,1)S(1)}, u32[]{:S(2)}) %copy-start.1) | copy-done | bytes 2228248
  71.3 2.8 %collective-permute-start.4 = (bf16[68,128,128]{2,1,0:T(8,128)(2,1)}, bf16[68,128,128]{2,1,0:T(8,128)(2,1)}, u32[]{:S(2)}, u32[]{:S(2)}) collective-permute-start(bf16[68,128,128]{2,1,0:T(8,128)(2,1)} %get-tuple-element.31.mine_ref), channel_id=1, source_target_pairs={{0,1},{1,0},{2,3},{3,2},{4,5},{5,4},{6,7},{7,6},{8,9},{9,8},{10,11... | collective-permute-start | bytes 6684680 | tf_op jit(solution)/shard_map/ppermute | solution.py:28
  74.1 0.0 copy-start.7
  74.1 0.0 copy-start.9
  74.2 3.9 %all-to-all-start.1 = ((bf16[32,272,128]{2,1,0:T(8,128)(2,1)}), bf16[32,272,128]{2,1,0:T(8,128)(2,1)S(1)}, u32[]{:S(2)}, u32[]{:S(2)}) async-start(bf16[32,272,128]{2,1,0:T(8,128)(2,1)} %copy-done.1), calls=%async_computation.1 | async-start | bytes 4456448 | tf_op jit(solution)/shard_map/all_to_all | solution.py:36
  78.0 0.4 collective-permute-done.4.theirs_ref
  78.4 8.1 %weight_gradients.1 = (bf16[4,64,2048]{2,1,0:T(8,128)(2,1)}, bf16[4,64,2048]{2,1,0:T(8,128)(2,1)}) custom-call(s32[4,32]{1,0:T(4,128)S(1)} %bitcast.22, s32[4,32]{1,0:T(4,128)S(1)} %bitcast.24, bf16[68,128,128]{2,1,0:T(8,128)(2,1)} %get-tuple-element.31.mine_ref, bf16[4,128,128]{2,1,0:T(8,128)(2,1)S(1)} %get-tuple-element.32.keep_ref, ...), custom_call_target="tpu_custom_call" | custom-call | flops 1000000 | bytes 100000 | tf_op jit(solution)/shard_map/weight_gradients/pallas_call | solution.py:305
  86.5 21.2 %all-to-all-done.1.parts_ref = bf16[32,272,128]{2,1,0:T(8,128)(2,1)S(1)} async-done(((bf16[32,272,128]{2,1,0:T(8,128)(2,1)}), bf16[32,272,128]{2,1,0:T(8,128)(2,1)S(1)}, u32[]{:S(2)}, u32[]{:S(2)}) %all-to-all-start.1) | async-done | bytes 2228256 | tf_op jit(solution)/shard_map/all_to_all | solution.py:36
  107.7 0.8 input_gradient.1
  108.5 9.1 %collective-permute-start.5 = (bf16[256,128]{1,0:T(8,128)(2,1)S(1)}, bf16[256,128]{1,0:T(8,128)(2,1)S(1)}, u32[]{:S(2)}, u32[]{:S(2)}) collective-permute-start(bf16[256,128]{1,0:T(8,128)(2,1)S(1)} %get-tuple-element.40), channel_id=1, source_target_pairs={{0,480},{32,0},{64,32},{96,64},{128,96},{160,128},{192,160},{224,1... | collective-permute-start | bytes 196616 | tf_op jit(solution)/shard_map/ppermute | solution.py:23
  117.6 0.8 section_outputs.1
  118.4 0.5 collective-permute-done.5
  118.9 0.6 copy.18
  119.5 0.6 copy.19
  (17 shorter events, 0.0 us)
Async XLA Ops:
  0.6 17.3 %collective-permute-start = (bf16[256,128]{1,0:T(8,128)(2,1)}, bf16[256,128]{1,0:T(8,128)(2,1)S(1)}, u32[]{:S(2)}, u32[]{:S(2)}) collective-permute-start(bf16[256,128]{1,0:T(8,128)(2,1)} %bitcast.29), channel_id=1, source_target_pairs={{0,32},{32,64},{64,96},{96,128},{128,160},{160,192},{192,224},{224... | collective-permute-start | bytes 196616 | tf_op jit(solution)/shard_map/ppermute | solution.py:23
  5.0 1.2 %copy-start.2 = (bf16[1,4,64,2048]{3,2,1,0:T(8,128)(2,1)S(1)}, bf16[1,4,64,2048]{3,2,1,0:T(8,128)(2,1)}, u32[]{:S(2)}) copy-start(bf16[1,4,64,2048]{3,2,1,0:T(8,128)(2,1)} %param.14) | copy-start | bytes 3145732
  6.3 1.2 %copy-start.3 = (bf16[1,4,64,2048]{3,2,1,0:T(8,128)(2,1)S(1)}, bf16[1,4,64,2048]{3,2,1,0:T(8,128)(2,1)}, u32[]{:S(2)}) copy-start(bf16[1,4,64,2048]{3,2,1,0:T(8,128)(2,1)} %param.15) | copy-start | bytes 3145732
  7.5 0.7 copy-start.6
  8.2 0.7 copy-start.8
  8.8 9.1 %copy-start.4 = (bf16[1,256,128]{2,1,0:T(8,128)(2,1)S(1)}, bf16[1,256,128]{2,1,0:T(8,128)(2,1)}, u32[]{:S(2)}) copy-start(bf16[1,256,128]{2,1,0:T(8,128)(2,1)} %param.11) | copy-start | bytes 196612
  8.8 9.1 %copy-start.5 = (bf16[1,256,128]{2,1,0:T(8,128)(2,1)S(1)}, bf16[1,256,128]{2,1,0:T(8,128)(2,1)}, u32[]{:S(2)}) copy-start(bf16[1,256,128]{2,1,0:T(8,128)(2,1)} %param.12) | copy-start | bytes 196612
  8.8 9.1 %copy-start.10 = (bf16[1,128]{1,0:T(2,128)(2,1)S(1)}, bf16[1,128]{1,0:T(2,128)(2,1)}, u32[]{:S(2)}) copy-start(bf16[1,128]{1,0:T(2,128)(2,1)} %gain_ref.3) | copy-start | bytes 772
  18.2 1.4 %copy-start = (bf16[32,272,128]{2,1,0:T(8,128)(2,1)}, bf16[32,272,128]{2,1,0:T(8,128)(2,1)S(1)}, u32[]{:S(2)}) copy-start(bf16[32,272,128]{2,1,0:T(8,128)(2,1)S(1)} %pack_chunks.1) | copy-start | bytes 6684676
  19.7 19.5 %copy-start.11 = (bf16[1,256,128]{2,1,0:T(8,128)(2,1)S(1)}, bf16[1,256,128]{2,1,0:T(8,128)(2,1)}, u32[]{:S(2)}) copy-start(bf16[1,256,128]{2,1,0:T(8,128)(2,1)} %param.10) | copy-start | bytes 196612
  19.7 40.0 %collective-permute-start.3 = (bf16[512,4096]{1,0:T(8,128)(2,1)}, bf16[512,4096]{1,0:T(8,128)(2,1)}, u32[]{:S(2)}, u32[]{:S(2)}) collective-permute-start(bf16[512,4096]{1,0:T(8,128)(2,1)} %densify.1.own_hbm), channel_id=1, source_target_pairs={{0,1},{1,0},{2,3},{3,2},{4,5},{5,4},{6,7},{7,6},{8,9},{9,8},{10,11... | collective-permute-start | bytes 12582920 | tf_op jit(solution)/shard_map/ppermute | solution.py:28
  26.1 33.5 %all-to-all-start = ((bf16[32,272,128]{2,1,0:T(8,128)(2,1)}), bf16[32,272,128]{2,1,0:T(8,128)(2,1)S(1)}, u32[]{:S(2)}, u32[]{:S(2)}) async-start(bf16[32,272,128]{2,1,0:T(8,128)(2,1)} %copy-done), calls=%async_computation | async-start | bytes 4456448 | tf_op jit(solution)/shard_map/all_to_all | solution.py:36
  30.0 11.1 %collective-permute-start.1 = (bf16[256,128]{1,0:T(8,128)(2,1)S(1)}, bf16[256,128]{1,0:T(8,128)(2,1)S(1)}, u32[]{:S(2)}, u32[]{:S(2)}) collective-permute-start(bf16[256,128]{1,0:T(8,128)(2,1)S(1)} %broadcast_select_fusion), channel_id=1, source_target_pairs={{0,480},{32,0},{64,32},{96,64},{128,96},{160,128},{192,160},{224,1... | collective-permute-start | bytes 196616 | tf_op jit(solution)/shard_map/ppermute | solution.py:23
  39.1 6.5 %collective-permute-start.2 = (bf16[256,128]{1,0:T(8,128)(2,1)S(1)}, bf16[256,128]{1,0:T(8,128)(2,1)S(1)}, u32[]{:S(2)}, u32[]{:S(2)}) collective-permute-start(bf16[256,128]{1,0:T(8,128)(2,1)S(1)} %bitcast.30), channel_id=1, source_target_pairs={{0,32},{32,64},{64,96},{96,128},{128,160},{160,192},{192,224},{224... | collective-permute-start | bytes 196616 | tf_op jit(solution)/shard_map/ppermute | solution.py:23
  69.9 1.4 %copy-start.1 = (bf16[32,272,128]{2,1,0:T(8,128)(2,1)}, bf16[32,272,128]{2,1,0:T(8,128)(2,1)S(1)}, u32[]{:S(2)}) copy-start(bf16[32,272,128]{2,1,0:T(8,128)(2,1)S(1)} %get-tuple-element.35) | copy-start | bytes 6684676
  71.3 7.1 %collective-permute-start.4 = (bf16[68,128,128]{2,1,0:T(8,128)(2,1)}, bf16[68,128,128]{2,1,0:T(8,128)(2,1)}, u32[]{:S(2)}, u32[]{:S(2)}) collective-permute-start(bf16[68,128,128]{2,1,0:T(8,128)(2,1)} %get-tuple-element.31.mine_ref), channel_id=1, source_target_pairs={{0,1},{1,0},{2,3},{3,2},{4,5},{5,4},{6,7},{7,6},{8,9},{9,8},{10,11... | collective-permute-start | bytes 6684680 | tf_op jit(solution)/shard_map/ppermute | solution.py:28
  74.1 4.3 %copy-start.7 = (s32[1,4,32]{2,1,0:T(4,128)S(1)}, s32[1,4,32]{2,1,0:T(4,128)}, u32[]{:S(2)}) copy-start(s32[1,4,32]{2,1,0:T(4,128)} %param.16) | copy-start | bytes 1540
  74.1 4.3 %copy-start.9 = (s32[1,4,32]{2,1,0:T(4,128)S(1)}, s32[1,4,32]{2,1,0:T(4,128)}, u32[]{:S(2)}) copy-start(s32[1,4,32]{2,1,0:T(4,128)} %param.17) | copy-start | bytes 1540
  74.2 33.5 %all-to-all-start.1 = ((bf16[32,272,128]{2,1,0:T(8,128)(2,1)}), bf16[32,272,128]{2,1,0:T(8,128)(2,1)S(1)}, u32[]{:S(2)}, u32[]{:S(2)}) async-start(bf16[32,272,128]{2,1,0:T(8,128)(2,1)} %copy-done.1), calls=%async_computation.1 | async-start | bytes 4456448 | tf_op jit(solution)/shard_map/all_to_all | solution.py:36
  108.5 10.4 %collective-permute-start.5 = (bf16[256,128]{1,0:T(8,128)(2,1)S(1)}, bf16[256,128]{1,0:T(8,128)(2,1)S(1)}, u32[]{:S(2)}, u32[]{:S(2)}) collective-permute-start(bf16[256,128]{1,0:T(8,128)(2,1)S(1)} %get-tuple-element.40), channel_id=1, source_target_pairs={{0,480},{32,0},{64,32},{96,64},{128,96},{160,128},{192,160},{224,1... | collective-permute-start | bytes 196616 | tf_op jit(solution)/shard_map/ppermute | solution.py:23

commit v2 on v1

--- a/solution.py
+++ b/solution.py
@@ -9,6 +9,7 @@
 
 eps = 1e-05
 LANES = 128
+MAIN_VMEM = 24
 EXTRA = 16
 F32 = jnp.float32
 BF16 = jnp.bfloat16
@@ -36,28 +37,85 @@
     return lax.all_to_all(chunks, "dp", 0, 0, tiled=True)
 
 
-def pack_kernel(odd_ref, base_ref, cot_base_ref, cot_part_ref, gain_ref, out_ref):
-    count, rows, _ = out_ref.shape
+def pack_kernel(odd_ref, cot_base_hbm, cot_part_hbm, gain_hbm, out_ref, cot_base_ref, cot_part_ref, gain_ref, chunk, sems, in_sems):
+    count = out_ref.shape[0]
+    loads = [
+        pltpu.make_async_copy(source, target, in_sems.at[n])
+        for n, (source, target) in enumerate(
+            ((cot_base_hbm, cot_base_ref), (cot_part_hbm, cot_part_ref), (gain_hbm, gain_ref))
+        )
+    ]
+    for load in loads:
+        load.start()
+    for load in loads:
+        load.wait()
+    half = cot_base_ref.shape[0] // 2
+    odd = odd_ref[0] == 1
+    copies = []
+    for n in range(2):
+        at = pl.ds(n * half, half)
+        chunk[n, :half, :] = jnp.where(odd, cot_base_ref[at, :], cot_part_ref[at, :])
+        chunk[n, half:, :] = jnp.broadcast_to(gain_ref[...].astype(F32), (EXTRA, LANES)).astype(BF16)
+    for j in range(count):
+        copies.append(
+            pltpu.make_async_copy(
+                chunk.at[j % 2], out_ref.at[j, pl.ds(half, half + EXTRA)], sems.at[j]
+            )
+        )
+        copies[-1].start()
+    for copy in copies:
+        copy.wait()
+
+
+def pack(odd, cot_base, cot_part, gain, count):
+    tokens = cot_base.shape[0]
+    return pl.pallas_call(
+        pack_kernel,
+        out_shape=jax.ShapeDtypeStruct((count, tokens + EXTRA, LANES), BF16),
+        in_specs=[SMEM, HBM, HBM, HBM],
+        out_specs=HBM,
+        scratch_shapes=[
+            pltpu.VMEM(cot_base.shape, BF16),
+            pltpu.VMEM(cot_part.shape, BF16),
+            pltpu.VMEM(gain.shape, BF16),
+            pltpu.VMEM((2, tokens // 2 + EXTRA, LANES), BF16),
+            pltpu.SemaphoreType.DMA((count,)),
+            pltpu.SemaphoreType.DMA((3,)),
+        ],
+        compiler_params=pltpu.CompilerParams(vmem_limit_bytes=60 * 1024 * 1024),
+        cost_estimate=pl.CostEstimate(flops=1_000_000, bytes_accessed=1_500_000, transcendentals=0),
+        name="pack_cotangent",
+    )(odd[None], cot_base, cot_part, gain)
+
+
+def pack_base_kernel(base_ref, packed_ref, out_ref, sems):
+    count = out_ref.shape[0]
     half = base_ref.shape[0] // 2
-    odd = odd_ref[0] == 1
-    gain = jnp.broadcast_to(gain_ref[...].astype(F32), (EXTRA, LANES)).astype(BF16)
+    copies = []
     for j in range(count):
-        at = pl.ds((j % 2) * half, half)
-        out_ref[j, :half, :] = base_ref[at, :]
-        out_ref[j, half : 2 * half, :] = jnp.where(odd, cot_base_ref[at, :], cot_part_ref[at, :])
-        out_ref[j, 2 * half :, :] = gain
-
-
-def pack(odd, base, cot_base, cot_part, gain, count):
-    return pl.pallas_call(
-        pack_kernel,
-        out_shape=jax.ShapeDtypeStruct((count, base.shape[0] + EXTRA, LANES), BF16),
-        in_specs=[SMEM, VMEM, VMEM, VMEM, VMEM],
-        out_specs=VMEM,
-        compiler_params=PARAMS,
-        cost_estimate=pl.CostEstimate(flops=1_000_000, bytes_accessed=2_500_000, transcendentals=0),
-        name="pack_chunks",
-    )(odd[None], base, cot_base, cot_part, gain)
+        copies.append(
+            pltpu.make_async_copy(
+                base_ref.at[pl.ds((j % 2) * half, half)], out_ref.at[j, pl.ds(0, half)], sems.at[j]
+            )
+        )
+        copies[-1].start()
+    for copy in copies:
+        copy.wait()
+
+
+def pack_base(base, packed):
+    count = packed.shape[0]
+    return pl.pallas_call(
+        pack_base_kernel,
+        out_shape=jax.ShapeDtypeStruct(packed.shape, BF16),
+        in_specs=[VMEM, HBM],
+        out_specs=HBM,
+        scratch_shapes=[pltpu.SemaphoreType.DMA((count,))],
+        input_output_aliases={1: 0},
+        compiler_params=pltpu.CompilerParams(vmem_limit_bytes=16 * 1024 * 1024),
+        cost_estimate=pl.CostEstimate(flops=1_000, bytes_accessed=1_000_000, transcendentals=0),
+        name="pack_base",
+    )(base, packed)
 
 
 def merge_tiles(tile0, tile1, turned0, turned1, kept0, kept1, lower):
@@ -75,16 +133,14 @@
     return pl.ds(pl.multiple_of(n * LANES, LANES), LANES)
 
 
-def densify_kernel(idx_up, idx_down, up_ref, down_ref, out_ref, dense, sems):
+def densify_kernel(idx_up, idx_down, up_ref, down_ref, after_ref, dense_up, dense_down):
     hblk, blk, wide = up_ref.shape
     kept = idx_up.shape[1]
-    tiles = out_ref.shape[1] // LANES
-    units = hblk * blk
+    tiles = dense_up.shape[1] // LANES
     lower = lax.broadcasted_iota(jnp.int32, (1, LANES), 1) < blk
-    copies = []
-    for which, (idx, src) in enumerate(((idx_up, up_ref), (idx_down, down_ref))):
-
-        def step(j, ats, which=which, idx=idx, src=src):
+    for idx, src, dense in ((idx_up, up_ref, dense_up), (idx_down, down_ref, dense_down)):
+
+        def step(j, ats, idx=idx, src=src, dense=dense):
             plans, next_ats = [], []
             for c in range(hblk):
                 p0 = jnp.minimum(ats[c], kept - 1)
@@ -103,29 +159,23 @@
                 for (tile0, tile1), (p0, m0, p1, m1) in zip(loaded, plans)
             ]
             for c in range(hblk):
-                dense[pl.ds(which * units + c * blk, blk), tile_at(j)] = merged[c]
+                dense[pl.ds(c * blk, blk), tile_at(j)] = merged[c]
             return tuple(next_ats)
 
         lax.fori_loop(0, tiles, step, (jnp.int32(0),) * hblk, unroll=2)
-        rows = pl.ds(which * units, units)
-        copies.append(pltpu.make_async_copy(dense.at[rows], out_ref.at[rows], sems.at[which]))
-        copies[-1].start()
-    for copy in copies:
-        copy.wait()
-
-
-def densify(idx_up, idx_down, up, down, width):
+
+
+def densify(idx_up, idx_down, up, down, width, earlier):
     hblk, blk, _ = up.shape
     return pl.pallas_call(
         densify_kernel,
-        out_shape=jax.ShapeDtypeStruct((2 * hblk * blk, width), BF16),
-        in_specs=[SMEM, SMEM, VMEM, VMEM],
-        out_specs=HBM,
-        scratch_shapes=[pltpu.VMEM((2 * hblk * blk, width), BF16), pltpu.SemaphoreType.DMA((2,))],
-        compiler_params=PARAMS,
+        out_shape=[jax.ShapeDtypeStruct((hblk * blk, width), BF16)] * 2,
+        in_specs=[SMEM, SMEM, VMEM, VMEM, pl.BlockSpec(memory_space=pl.ANY)],
+        out_specs=[VMEM, VMEM],
+        compiler_params=pltpu.CompilerParams(vmem_limit_bytes=20 * 1024 * 1024),
         cost_estimate=pl.CostEstimate(flops=10_000_000, bytes_accessed=6_291_456, transcendentals=0),
         name="densify",
-    )(idx_up, idx_down, up, down)
+    )(idx_up, idx_down, up, down, earlier)
 
 
 def dot_nt(a, b):
@@ -144,58 +194,47 @@
 
 
 def main_kernel(
-    rows_ref, own_hbm, other_hbm, back_hbm, swap_ref, keep_ref, weights, back_ref, in_sems, out_sems
+    rows_ref, own_up, own_down, other_up, other_down, spent_ref, back_hbm, inverse_ref, give_ref, keep_ref, tiles_ref, weights, back_ref, in_sems, out_sems
 ):
     count = rows_ref.shape[0]
     tokens = (rows_ref.shape[1] - EXTRA) // 2
     width = count * LANES
-    units = own_hbm.shape[0] // 2
-    loads = []
-    for n, (source, which) in enumerate(((own_hbm, 0), (other_hbm, 0), (own_hbm, 1), (other_hbm, 1))):
-        loads.append(
-            pltpu.make_async_copy(
-                source.at[pl.ds(which * units, units)], weights.at[n], in_sems.at[n]
-            )
-        )
-        loads[-1].start()
+    units = own_up.shape[0]
+    per = units // LANES
+    loads = [
+        pltpu.make_async_copy(source, weights.at[n], in_sems.at[n])
+        for n, source in enumerate((own_up, own_down, other_up, other_down))
+    ]
+    for load in loads:
+        load.start()
     squares = jnp.zeros((tokens, LANES), F32)
     for j in range(count):
         x = rows_ref[j, :tokens, :].astype(F32)
         squares = squares + x * x
     mean_square = jnp.sum(squares, axis=-1, keepdims=True) / width
     inverse = 1.0 / jnp.sqrt(mean_square + eps)
+    inverse_ref[...] = jnp.broadcast_to(inverse, inverse_ref.shape)
     for j in range(count):
         x = rows_ref[j, :tokens, :].astype(F32)
         gain = rows_ref[j, 2 * tokens :, :].astype(F32)[:1]
-        swap_ref[j] = (x * inverse * gain).astype(BF16)
-        swap_ref[count + j] = rows_ref[j, tokens : 2 * tokens, :]
-    normed = jnp.concatenate([swap_ref[j] for j in range(count)], axis=1)
-    g_rows = jnp.concatenate(
-        [rows_ref[j, tokens : 2 * tokens, :] for j in range(count)], axis=1
-    )
-    pres, g_hiddens = [], []
-    for n in range(2):
-        loads[n].wait()
-        pres.append(dot_nt(normed, weights[n]))
-    for n in range(2):
-        loads[2 + n].wait()
-        g_hiddens.append(dot_nt(g_rows, weights[2 + n]))
-    per = units // LANES
+        tiles_ref[j] = (x * inverse * gain).astype(BF16)
+    normed = jnp.concatenate([tiles_ref[j] for j in range(count)], axis=1)
+    g_rows = jnp.concatenate([rows_ref[j, tokens : 2 * tokens, :] for j in range(count)], axis=1)
     stat = jnp.zeros((tokens, 1), F32)
     hiddens, g_pres = [], []
-    for n, (pre, g_hidden) in enumerate(zip(pres, g_hiddens)):
+    for n, target in enumerate((keep_ref, give_ref)):
+        loads[2 * n].wait()
+        pre = dot_nt(normed, weights[2 * n])
+        loads[2 * n + 1].wait()
+        g_hidden = dot_nt(g_rows, weights[2 * n + 1])
         sig = 1.0 / (1.0 + jnp.exp(-pre))
         hidden = (pre * sig).astype(BF16)
         g_pre = (g_hidden * sig * (1.0 + pre * (1.0 - sig))).astype(BF16)
         stat = stat + jnp.sum(g_pre.astype(F32) * pre, axis=-1, keepdims=True)
         for k in range(per):
             at = slice(k * LANES, (k + 1) * LANES)
-            if n == 0:
-                keep_ref[k] = hidden[:, at]
-                keep_ref[per + k] = g_pre[:, at]
-            else:
-                swap_ref[2 * count + k] = hidden[:, at]
-                swap_ref[2 * count + per + k] = g_pre[:, at]
+            target[k] = hidden[:, at]
+            target[per + k] = g_pre[:, at]
         hiddens.append(hidden)
         g_pres.append(g_pre)
     stat_high, stat_low, _ = split3(stat)
@@ -208,9 +247,9 @@
     stores = []
     for n, s in enumerate(range(0, width, step)):
         back = dot_nn(g_pres[0], weights[0, :, s : s + step]) + dot_nn(
-            g_pres[1], weights[1, :, s : s + step]
+            g_pres[1], weights[2, :, s : s + step]
         )
-        ffn = dot_nn(hiddens[0], weights[2, :, s : s + step]) + dot_nn(
+        ffn = dot_nn(hiddens[0], weights[1, :, s : s + step]) + dot_nn(
             hiddens[1], weights[3, :, s : s + step]
         )
         for k in range(step // LANES):
@@ -226,42 +265,70 @@
         store.wait()
 
 
-def main(rows, own, other):
+def main(rows, own, other, spent):
     count = rows.shape[0]
     tokens = (rows.shape[1] - EXTRA) // 2
-    units, width = own.shape[0] // 2, own.shape[1]
+    units, width = own[0].shape
     per = units // LANES
     return pl.pallas_call(
         main_kernel,
         out_shape=(
-            jax.ShapeDtypeStruct(rows.shape, BF16),
-            jax.ShapeDtypeStruct((2 * count + 2 * per, tokens, LANES), BF16),
+            jax.ShapeDtypeStruct(spent.shape, BF16),
+            jax.ShapeDtypeStruct((tokens, LANES), F32),
+            jax.ShapeDtypeStruct((2 * per, tokens, LANES), BF16),
             jax.ShapeDtypeStruct((2 * per, tokens, LANES), BF16),
         ),
-        in_specs=[VMEM, HBM, HBM],
-        out_specs=[HBM, VMEM, VMEM],
+        in_specs=[VMEM] + [HBM] * 5,
+        out_specs=[HBM, VMEM, VMEM, VMEM],
         scratch_shapes=[
+            pltpu.VMEM((count, tokens, LANES), BF16),
             pltpu.VMEM((4, units, width), BF16),
-            pltpu.VMEM(rows.shape, BF16),
+            pltpu.VMEM(spent.shape, BF16),
             pltpu.SemaphoreType.DMA((4,)),
             pltpu.SemaphoreType.DMA((width // 1024,)),
         ],
-        compiler_params=PARAMS,
+        input_output_aliases={5: 0},
+        compiler_params=pltpu.CompilerParams(vmem_limit_bytes=MAIN_VMEM * 1024 * 1024),
         cost_estimate=pl.CostEstimate(flops=2_200_000_000, bytes_accessed=16_000_000, transcendentals=65_536),
         name="forward_backward",
-    )(rows, own, other)
-
-
-def grads_kernel(idx_up, idx_down, mine_ref, keep_ref, theirs_ref, up_ref, down_ref, dense):
+    )(rows, *own, *other, spent)
+
+
+def normalize_kernel(rows_ref, inverse_ref, tiles_ref):
+    count = rows_ref.shape[0]
+    tokens = (rows_ref.shape[1] - EXTRA) // 2
+    inverse = inverse_ref[...]
+    for j in range(count):
+        x = rows_ref[j, :tokens, :].astype(F32)
+        gain = rows_ref[j, 2 * tokens :, :].astype(F32)[:1]
+        tiles_ref[j] = (x * inverse * gain).astype(BF16)
+        tiles_ref[count + j] = rows_ref[j, tokens : 2 * tokens, :]
+
+
+def normalize(rows, inverse):
+    count = rows.shape[0]
+    tokens = (rows.shape[1] - EXTRA) // 2
+    return pl.pallas_call(
+        normalize_kernel,
+        out_shape=jax.ShapeDtypeStruct((2 * count, tokens, LANES), BF16),
+        in_specs=[VMEM, VMEM],
+        out_specs=VMEM,
+        compiler_params=pltpu.CompilerParams(vmem_limit_bytes=12 * 1024 * 1024),
+        cost_estimate=pl.CostEstimate(flops=4_000_000, bytes_accessed=4_000_000, transcendentals=0),
+        name="normalize",
+    )(rows, inverse)
+
+
+def grads_kernel(idx_up, idx_down, mine_ref, keep_ref, theirs_ref, given_ref, up_ref, down_ref, dense):
     hblk, blk, wide = up_ref.shape
     per = hblk * blk // LANES
-    count = (mine_ref.shape[0] - 2 * per) // 2
+    count = mine_ref.shape[0] // 2
     lower = lax.broadcasted_iota(jnp.int32, (1, LANES), 1) < blk
     group = 8
 
     def left(n):
         tiles = [
-            jnp.concatenate([keep_ref[n * per + k], theirs_ref[2 * count + n * per + k]], axis=0)
+            jnp.concatenate([keep_ref[n * per + k], given_ref[n * per + k]], axis=0)
             for k in range(per)
         ]
         return jnp.concatenate(tiles, axis=1)
@@ -300,56 +367,80 @@
         lax.fori_loop(0, wide // LANES, step, 0, unroll=2)
 
 
-def grads(idx_up, idx_down, mine, keep, theirs, shape, width):
+def grads(idx_up, idx_down, mine, keep, theirs, given, shape, width):
     hblk, blk, _ = shape
     return pl.pallas_call(
         grads_kernel,
         out_shape=(jax.ShapeDtypeStruct(shape, BF16), jax.ShapeDtypeStruct(shape, BF16)),
-        in_specs=[SMEM, SMEM, VMEM, VMEM, VMEM],
+        in_specs=[SMEM, SMEM, VMEM, VMEM, VMEM, VMEM],
         out_specs=[VMEM, VMEM],
         scratch_shapes=[pltpu.VMEM((hblk * blk, width), BF16)],
         compiler_params=PARAMS,
         cost_estimate=pl.CostEstimate(flops=1_000_000, bytes_accessed=100_000, transcendentals=0),
         name="weight_gradients",
-    )(idx_up, idx_down, mine, keep, theirs)
-
-
-def finish_kernel(width, parts_ref, base_ref, gain_ref, cot_ref, out_ref, gain_out_ref):
-    count = parts_ref.shape[0]
-    tokens = (parts_ref.shape[1] - EXTRA) // 2
+    )(idx_up, idx_down, mine, keep, theirs, given)
+
+
+def finish_kernel(width, parts_hbm, base_ref, gain_ref, cot_ref, out_ref, gain_out_ref, parts, riding_ref, sems):
+    count = parts_hbm.shape[0]
+    tokens = (parts_hbm.shape[1] - EXTRA) // 2
+    group = 8
+    riding_load = pltpu.make_async_copy(
+        parts_hbm.at[:, pl.ds(2 * tokens, EXTRA)], riding_ref, sems.at[count // group]
+    )
+    riding_load.start()
+    loads = []
+    for n in range(count // group):
+        at = pl.ds(n * group, group)
+        loads.append(
+            pltpu.make_async_copy(parts_hbm.at[at, pl.ds(0, tokens)], parts.at[at], sems.at[n])
+        )
+        loads[-1].start()
+    riding_load.wait()
+    row = lax.broadcasted_iota(jnp.int32, (LANES, LANES), 0)
+    stats, inverses = [], []
+    for half in range(2):
+        riding = jnp.zeros((EXTRA, LANES), F32)
+        for j in range(half, count, 2):
+            riding = riding + riding_ref[j].astype(F32)
+        first = riding_ref[half].astype(F32)
+        summed = (riding[0:1] + riding[1:2]) / width
+        inverse = first[2:3] + first[3:4] + first[4:5]
+        turned = jnp.transpose(jnp.where(row == 0, summed, jnp.where(row == 1, inverse, 0.0)))
+        stats.append(turned[:, 0:1])
+        inverses.append(turned[:, 1:2])
+    totals = [jnp.zeros((tokens, LANES), F32) for _ in range(2)]
+    for n, load in enumerate(loads):
+        load.wait()
+        for j in range(n * group, (n + 1) * group):
+            totals[j % 2] = totals[j % 2] + parts[j].astype(F32)
     gain = gain_ref[...].astype(F32)
     total_gain = jnp.zeros((1, LANES), F32)
     for half in range(2):
-        total = jnp.zeros((tokens, LANES), F32)
-        riding = jnp.zeros((EXTRA, LANES), F32)
-        for j in range(half, count, 2):
-            total = total + parts_ref[j, :tokens, :].astype(F32)
-            riding = riding + parts_ref[j, 2 * tokens :, :].astype(F32)
-        first = parts_ref[half, 2 * tokens :, :].astype(F32)
-        summed = (riding[0:1] + riding[1:2]) / width
-        inverse = first[2:3] + first[3:4] + first[4:5]
-        row = lax.broadcasted_iota(jnp.int32, (LANES, LANES), 0)
-        turned = jnp.transpose(jnp.where(row == 0, summed, jnp.where(row == 1, inverse, 0.0)))
-        stat = turned[:, 0:1]
-        inverse = turned[:, 1:2]
         at = pl.ds(half * tokens, tokens)
-        scaled = base_ref[at, :].astype(F32) * inverse
+        scaled = base_ref[at, :].astype(F32) * inverses[half]
         out_ref[at, :] = (
-            (total * gain - scaled * stat) * inverse + cot_ref[at, :].astype(F32)
+            (totals[half] * gain - scaled * stats[half]) * inverses[half] + cot_ref[at, :].astype(F32)
         ).astype(BF16)
-        total_gain = total_gain + jnp.sum(total * scaled, axis=0, keepdims=True)
+        total_gain = total_gain + jnp.sum(totals[half] * scaled, axis=0, keepdims=True)
     gain_out_ref[...] = total_gain
 
 
 def finish(parts, base, gain, cot, width):
+    count, rows, _ = parts.shape
     return pl.pallas_call(
         functools.partial(finish_kernel, width),
         out_shape=(
             jax.ShapeDtypeStruct(base.shape, BF16),
             jax.ShapeDtypeStruct((1, LANES), F32),
         ),
-        in_specs=[VMEM] * 4,
+        in_specs=[HBM, VMEM, VMEM, VMEM],
         out_specs=[VMEM] * 2,
+        scratch_shapes=[
+            pltpu.VMEM((count, (rows - EXTRA) // 2, LANES), BF16),
+            pltpu.VMEM((count, EXTRA, LANES), BF16),
+            pltpu.SemaphoreType.DMA((count // 8 + 1,)),
+        ],
         compiler_params=PARAMS,
         cost_estimate=pl.CostEstimate(flops=2_000_000, bytes_accessed=1_500_000, transcendentals=0),
         name="input_gradient",
@@ -399,22 +490,27 @@
     odd = lax.axis_index("pipe") % 2
 
     arrived_base = passed_along(sent_base[0], "pipe", 1)
-    own = densify(up_index[0], down_index[0], up_blocks[0], down_blocks[0], width)
-    packed = pack(odd, after(arrived_base, own), cot_base[0], cot_part[0], norm_gain, count)
+    packed = pack(odd, cot_base[0], cot_part[0], norm_gain, count)
+    packed = pack_base(arrived_base, packed)
     rows = exchange(packed)
-    other = other_core(after(own, packed))
+    own = densify(up_index[0], down_index[0], up_blocks[0], down_blocks[0], width, packed)
+    other = [other_core(array) for array in own]
     g_part = jnp.where(odd == 1, cot_base[0], jnp.zeros_like(cot_base[0]))
     back_part = passed_along(after(g_part, packed), "pipe", -1)
-    arrived_part = passed_along(after(sent_part[0], packed), "pipe", 1)
-    own_later, back_part, arrived_part = lax.optimization_barrier((own, back_part, arrived_part))
-
-    parts, swap, keep = main(rows, own_later, other)
-    theirs = other_core(swap)
+    rows, back_part = lax.optimization_barrier((rows, back_part))
+
+    parts, inverse, give, keep = main(rows, own, other, packed)
+    tiles = normalize(rows, inverse)
+    theirs = other_core(tiles)
+    given = other_core(give)
+    arrived_part = passed_along(after(sent_part[0], inverse), "pipe", 1)
     up_grad, down_grad = grads(
-        up_index[0], down_index[0], swap, keep, theirs, up_blocks.shape[1:], width
+        up_index[0], down_index[0], tiles, keep, theirs, given, up_blocks.shape[1:], width
     )
     part_rows = exchange(parts)
-    up_grad, down_grad, part_rows = lax.optimization_barrier((up_grad, down_grad, part_rows))
+    up_grad, down_grad, arrived_part, part_rows = lax.optimization_barrier(
+        (up_grad, down_grad, arrived_part, part_rows)
+    )
     base_gradient, gain_gradient = finish(part_rows, arrived_base, norm_gain, cot_base[0], width)
     back_base = passed_along(base_gradient, "pipe", -1)
     out_base, out_part = outputs(odd, part_rows, arrived_base, arrived_part)

time: 121 us -> 108 us (0.89)
  waiting for transfers between devices: 40.7 us -> 34.8 us
  local copies, waits for them, and re-layouts: 7.89 us -> 2.51 us
  starting transfers between devices: 41.5 us -> 36.3 us
  Pallas kernels: 29.3 us -> 33.1 us
    ppermute x4, starting transfers between devices: 24.5 us -> 13.6 us  [passed_along(): lax.ppermute(shard, axis, [(i, (i + by) % count) for i in range(count)])]
    all_to_all x2, waiting for transfers between devices: 35.2 us -> 25.8 us  [exchange(): return lax.all_to_all(chunks, 'dp', 0, 0, tiled=True)]
    all_to_all x2, starting transfers between devices: 7.71 us -> 14.1 us  [exchange(): return lax.all_to_all(chunks, 'dp', 0, 0, tiled=True)]
    unnamed x26 -> x16, local copies, waits for them, and re-layouts: 7.89 us -> 2.51 us
    ppermute x4, waiting for transfers between devices: 5.07 us -> 8.89 us  [passed_along(): lax.ppermute(shard, axis, [(i, (i + by) % count) for i in range(count)])]
    pallas_call x3 -> x5, Pallas kernels: 19.6 us -> 22.4 us  [the longest x1 9.74 us: densify(): pl.pallas_call(densify_kernel, out_shape=[jax.ShapeDtypeStruct((hblk * bl...]
    pallas_call x1, Pallas kernels: 8.08 us -> 6.38 us  [grads(): pl.pallas_call(grads_kernel, out_shape=(jax.ShapeDtypeStruct(shape, BF16)...]
    pallas_call x1, Pallas kernels: 0.82 us -> 2.45 us  [outputs(): pl.pallas_call(outputs_kernel, out_shape=(jax.ShapeDtypeStruct(base.shape...]
  transfers between devices with their start and end apart: 8 -> 10, of which waited for: 5 -> 4; matrix products, arithmetic and copies ran while one was open for 0% -> 0% of each run, Pallas kernels for 15% -> 20%
where the time goes in v2:
time: 108 us
  starting transfers between devices  36.3 us (34%)
  waiting for transfers between devices  34.8 us (32%)
  Pallas kernels  33.1 us (31%)
  local copies, waits for them, and re-layouts  2.51 us (2%)
    all_to_all x2, waiting for transfers between devices, exchange(): return lax.all_to_all(chunks, 'dp', 0, 0, tiled=True)  25.8 us
    all_to_all x2, starting transfers between devices, exchange(): return lax.all_to_all(chunks, 'dp', 0, 0, tiled=True)  14.1 us
    ppermute x4, starting transfers between devices, passed_along(): lax.ppermute(shard, axis, [(i, (i + by) % count) for i in range(count)])  13.6 us
    pallas_call x1, Pallas kernels, densify(): pl.pallas_call(densify_kernel, out_shape=[jax.ShapeDtypeStruct((hblk * bl...  9.74 us
    ppermute x4, waiting for transfers between devices, passed_along(): lax.ppermute(shard, axis, [(i, (i + by) % count) for i in range(count)])  8.89 us
    pallas_call x1, Pallas kernels, main(): pl.pallas_call(main_kernel, out_shape=(jax.ShapeDtypeStruct(spent.shape,...  8.83 us
    ppermute x4, starting transfers between devices, other_core(): return lax.ppermute(shard, 'dp', [(i, i ^ 1) for i in range(count)])  8.64 us
    pallas_call x1, Pallas kernels, grads(): pl.pallas_call(grads_kernel, out_shape=(jax.ShapeDtypeStruct(shape, BF16)...  6.38 us
  transfers between devices with their start and end apart: 10, of which 4 were waited for; matrix products, arithmetic and copies ran while one was open for 0% of the time, Pallas kernels for 20%

profile of v2, /device:TPU:1, one launch (start us, length us, event | category | flops | bytes accessed | tf_op | source)
XLA Modules:
  0.0 107.6 jit_solution(8812396981583895613)
XLA Ops:
  0.6 4.4 %collective-permute-start = (bf16[256,128]{1,0:T(8,128)(2,1)}, bf16[256,128]{1,0:T(8,128)(2,1)S(1)}, u32[]{:S(2)}, u32[]{:S(2)}) collective-permute-start(bf16[256,128]{1,0:T(8,128)(2,1)} %bitcast.29), channel_id=1, source_target_pairs={{0,32},{32,64},{64,96},{96,128},{128,160},{160,192},{192,224},{224... | collective-permute-start | bytes 196616 | tf_op jit(solution)/shard_map/ppermute | solution.py:24
  5.0 2.2 %pack_cotangent.1.packed_ref = bf16[32,272,128]{2,1,0:T(8,128)(2,1)} custom-call(s32[1]{0:T(128)} %bitcast.odd_ref, bf16[256,128]{1,0:T(8,128)(2,1)} %bitcast.18, bf16[256,128]{1,0:T(8,128)(2,1)} %bitcast.24, bf16[1,128]{1,0:T(2,128)(2,1)} %gain_ref.1), custom_call_target="tpu_custom_call" | custom-call | flops 1000000 | bytes 1500000 | tf_op jit(solution)/shard_map/pack_cotangent/pallas_call | solution.py:72
  7.3 7.2 %collective-permute-done.base_ref = bf16[256,128]{1,0:T(8,128)(2,1)S(1)} collective-permute-done((bf16[256,128]{1,0:T(8,128)(2,1)}, bf16[256,128]{1,0:T(8,128)(2,1)S(1)}, u32[]{:S(2)}, u32[]{:S(2)}) %collective-permute-start) | collective-permute-done | bytes 65568 | tf_op jit(solution)/shard_map/ppermute | solution.py:24
  14.4 1.3 %pack_base.1.after_ref.spent_ref = bf16[32,272,128]{2,1,0:T(8,128)(2,1)} custom-call(bf16[256,128]{1,0:T(8,128)(2,1)S(1)} %collective-permute-done.base_ref, bf16[32,272,128]{2,1,0:T(8,128)(2,1)} %pack_cotangent.1.packed_ref), custom_call_target="tpu_custom_call", output_to_operand_aliasing={{}: (1, {})} | custom-call | flops 1000 | bytes 1000000 | tf_op jit(solution)/shard_map/pack_base/pallas_call | solution.py:108
  15.8 0.0 copy-start
  15.8 0.0 copy-start.3
  15.8 0.0 copy-start.4
  15.8 8.8 %all-to-all-start = ((bf16[32,272,128]{2,1,0:T(8,128)(2,1)}), bf16[32,272,128]{2,1,0:T(8,128)(2,1)S(1)}, u32[]{:S(2)}, u32[]{:S(2)}) async-start(bf16[32,272,128]{2,1,0:T(8,128)(2,1)} %pack_base.1.after_ref.spent_ref), calls=%async_computation | async-start | bytes 4456448 | tf_op jit(solution)/shard_map/all_to_all | solution.py:37
  24.6 0.0 copy-start.1
  24.6 1.2 %copy-done.1 = bf16[1,4,64,2048]{3,2,1,0:T(8,128)(2,1)S(1)} copy-done((bf16[1,4,64,2048]{3,2,1,0:T(8,128)(2,1)S(1)}, bf16[1,4,64,2048]{3,2,1,0:T(8,128)(2,1)}, u32[]{:S(2)}) %copy-start.1) | copy-done | bytes 1048600
  25.8 9.7 %densify.1 = (bf16[256,4096]{1,0:T(8,128)(2,1)}, bf16[256,4096]{1,0:T(8,128)(2,1)}) custom-call(s32[4,32]{1,0:T(4,128)S(1)} %bitcast.20, s32[4,32]{1,0:T(4,128)S(1)} %bitcast.22, bf16[4,64,2048]{2,1,0:T(8,128)(2,1)S(1)} %bitcast.16, bf16[4,64,2048]{2,1,0:T(8,128)(2,1)S(1)} %bitcast.17, bf16[32,272,128]{2,1,0:T(8,128)(2,1)} %pack_base.1.after_ref.spent_ref), custom_call_target="tpu_custom_call" | custom-call | flops 10000000 | bytes 6291456 | tf_op jit(solution)/shard_map/densify/pallas_call | solution.py:170
  35.6 2.1 %collective-permute-start.2 = (bf16[256,4096]{1,0:T(8,128)(2,1)}, bf16[256,4096]{1,0:T(8,128)(2,1)}, u32[]{:S(2)}, u32[]{:S(2)}) collective-permute-start(bf16[256,4096]{1,0:T(8,128)(2,1)} %get-tuple-element.29.own_up), channel_id=1, source_target_pairs={{0,1},{1,0},{2,3},{3,2},{4,5},{5,4},{6,7},{7,6},{8,9},{9,8},{10,11... | collective-permute-start | bytes 6291464 | tf_op jit(solution)/shard_map/ppermute | solution.py:29
  37.7 2.2 %collective-permute-start.3 = (bf16[256,4096]{1,0:T(8,128)(2,1)}, bf16[256,4096]{1,0:T(8,128)(2,1)}, u32[]{:S(2)}, u32[]{:S(2)}) collective-permute-start(bf16[256,4096]{1,0:T(8,128)(2,1)} %get-tuple-element.30.own_down), channel_id=1, source_target_pairs={{0,1},{1,0},{2,3},{3,2},{4,5},{5,4},{6,7},{7,6},{8,9},{9,8},{10,11... | collective-permute-start | bytes 6291464 | tf_op jit(solution)/shard_map/ppermute | solution.py:29
  39.9 3.6 %collective-permute-start.1 = (bf16[256,128]{1,0:T(8,128)(2,1)S(1)}, bf16[256,128]{1,0:T(8,128)(2,1)S(1)}, u32[]{:S(2)}, u32[]{:S(2)}) collective-permute-start(bf16[256,128]{1,0:T(8,128)(2,1)S(1)} %broadcast_select_fusion), channel_id=1, source_target_pairs={{0,480},{32,0},{64,32},{96,64},{128,96},{160,128},{192,160},{224,1... | collective-permute-start | bytes 196616 | tf_op jit(solution)/shard_map/ppermute | solution.py:24
  43.6 1.7 %collective-permute-done.1 = bf16[256,128]{1,0:T(8,128)(2,1)S(1)} collective-permute-done((bf16[256,128]{1,0:T(8,128)(2,1)S(1)}, bf16[256,128]{1,0:T(8,128)(2,1)S(1)}, u32[]{:S(2)}, u32[]{:S(2)}) %collective-permute-start.1) | collective-permute-done | bytes 65568 | tf_op jit(solution)/shard_map/ppermute | solution.py:24
  45.3 9.0 %all-to-all-done.rows_ref = bf16[32,272,128]{2,1,0:T(8,128)(2,1)S(1)} async-done(((bf16[32,272,128]{2,1,0:T(8,128)(2,1)}), bf16[32,272,128]{2,1,0:T(8,128)(2,1)S(1)}, u32[]{:S(2)}, u32[]{:S(2)}) %all-to-all-start) | async-done | bytes 2228256 | tf_op jit(solution)/shard_map/all_to_all | solution.py:37
  54.3 0.0 collective-permute-done.2.other_up
  54.3 8.8 %forward_backward.1 = (bf16[32,272,128]{2,1,0:T(8,128)(2,1)}, f32[128,128]{1,0:T(8,128)S(1)}, bf16[4,128,128]{2,1,0:T(8,128)(2,1)S(1)}, bf16[4,128,128]{2,1,0:T(8,128)(2,1)S(1)}) custom-call(bf16[32,272,128]{2,1,0:T(8,128)(2,1)S(1)} %all-to-all-done.rows_ref, bf16[256,4096]{1,0:T(8,128)(2,1)} %get-tuple-element.29.own_up, ...), custom_call_target="tpu_custom_call", output_to_operand_aliasing={{0}: (5, {})} | custom-call | flops 2200000000 | bytes 16000000 | tf_op jit(solution)/shard_map/forward_backward/pallas_call | solution.py:273
  63.1 5.3 %all-to-all-start.1 = ((bf16[32,272,128]{2,1,0:T(8,128)(2,1)}), bf16[32,272,128]{2,1,0:T(8,128)(2,1)}, u32[]{:S(2)}, u32[]{:S(2)}) async-start(bf16[32,272,128]{2,1,0:T(8,128)(2,1)} %get-tuple-element.37), calls=%async_computation.1 | async-start | bytes 4456448 | tf_op jit(solution)/shard_map/all_to_all | solution.py:37
  68.4 0.0 copy-start.6
  68.4 0.3 normalize.1.mine_ref
  68.7 2.3 %collective-permute-start.4 = (bf16[64,128,128]{2,1,0:T(8,128)(2,1)S(1)}, bf16[64,128,128]{2,1,0:T(8,128)(2,1)S(1)}, u32[]{:S(2)}, u32[]{:S(2)}) collective-permute-start(bf16[64,128,128]{2,1,0:T(8,128)(2,1)S(1)} %normalize.1.mine_ref), channel_id=1, source_target_pairs={{0,1},{1,0},{2,3},{3,2},{4,5},{5,4},{6,7},{7,6},{8,9},{9,8},{10,11... | collective-permute-start | bytes 6291464 | tf_op jit(solution)/shard_map/ppermute | solution.py:29
  71.0 2.0 %collective-permute-start.5 = (bf16[4,128,128]{2,1,0:T(8,128)(2,1)S(1)}, bf16[4,128,128]{2,1,0:T(8,128)(2,1)S(1)}, u32[]{:S(2)}, u32[]{:S(2)}) collective-permute-start(bf16[4,128,128]{2,1,0:T(8,128)(2,1)S(1)} %get-tuple-element.33), channel_id=1, source_target_pairs={{0,1},{1,0},{2,3},{3,2},{4,5},{5,4},{6,7},{7,6},{8,9},{9,8},{10,11... | collective-permute-start | bytes 393224 | tf_op jit(solution)/shard_map/ppermute | solution.py:29
  73.0 1.9 %collective-permute-start.6 = (bf16[256,128]{1,0:T(8,128)(2,1)S(1)}, bf16[256,128]{1,0:T(8,128)(2,1)S(1)}, u32[]{:S(2)}, u32[]{:S(2)}) collective-permute-start(bf16[256,128]{1,0:T(8,128)(2,1)S(1)} %bitcast.30), channel_id=1, source_target_pairs={{0,32},{32,64},{64,96},{96,128},{128,160},{160,192},{192,224},{224... | collective-permute-start | bytes 196616 | tf_op jit(solution)/shard_map/ppermute | solution.py:24
  75.0 0.0 copy-start.5
  75.0 6.4 %weight_gradients.1 = (bf16[4,64,2048]{2,1,0:T(8,128)(2,1)}, bf16[4,64,2048]{2,1,0:T(8,128)(2,1)}) custom-call(s32[4,32]{1,0:T(4,128)S(1)} %bitcast.21, s32[4,32]{1,0:T(4,128)S(1)} %bitcast.23, bf16[64,128,128]{2,1,0:T(8,128)(2,1)S(1)} %normalize.1.mine_ref, bf16[4,128,128]{2,1,0:T(8,128)(2,1)S(1)} %get-tuple-element.32.keep_ref, ...), custom_call_target="tpu_custom_call" | custom-call | flops 1000000 | bytes 100000 | tf_op jit(solution)/shard_map/weight_gradients/pallas_call | solution.py:372
  81.4 16.9 %all-to-all-done.1.parts_ref.parts_hbm = bf16[32,272,128]{2,1,0:T(8,128)(2,1)} async-done(((bf16[32,272,128]{2,1,0:T(8,128)(2,1)}), bf16[32,272,128]{2,1,0:T(8,128)(2,1)}, u32[]{:S(2)}, u32[]{:S(2)}) %all-to-all-start.1) | async-done | bytes 2228256 | tf_op jit(solution)/shard_map/all_to_all | solution.py:37
  98.3 1.9 %input_gradient.1 = (bf16[256,128]{1,0:T(8,128)(2,1)S(1)}, f32[1,128]{1,0:T(1,128)}) custom-call(bf16[32,272,128]{2,1,0:T(8,128)(2,1)} %all-to-all-done.1.parts_ref.parts_hbm, bf16[256,128]{1,0:T(8,128)(2,1)S(1)} %collective-permute-done.base_ref, bf16[1,128]{1,0:T(2,128)(2,1)S(1)} %copy-done.5, bf16[256,128]{1,0:T(8,128)(2,1)S(1)} %bitcast.19), custom_call_target="tpu_custom_call" | custom-call | flops 2000000 | bytes 1500000 | tf_op jit(solution)/shard_map/input_gradient/pallas_call | solution.py:431
  100.2 3.6 %collective-permute-start.7 = (bf16[256,128]{1,0:T(8,128)(2,1)S(1)}, bf16[256,128]{1,0:T(8,128)(2,1)S(1)}, u32[]{:S(2)}, u32[]{:S(2)}) collective-permute-start(bf16[256,128]{1,0:T(8,128)(2,1)S(1)} %get-tuple-element.42), channel_id=1, source_target_pairs={{0,480},{32,0},{64,32},{96,64},{128,96},{160,128},{192,160},{224,1... | collective-permute-start | bytes 196616 | tf_op jit(solution)/shard_map/ppermute | solution.py:24
  103.9 2.4 %section_outputs.1 = (bf16[256,128]{1,0:T(8,128)(2,1)}, bf16[256,128]{1,0:T(8,128)(2,1)}) custom-call(s32[1]{0:T(128)} %bitcast.odd_ref, bf16[32,272,128]{2,1,0:T(8,128)(2,1)} %all-to-all-done.1.parts_ref.parts_hbm, bf16[256,128]{1,0:T(8,128)(2,1)S(1)} %collective-permute-done.base_ref, bf16[256,128]{1,0:T(8,128)(2,1)S(1)} %collective-permute-done.6.part_ref), custom_call_target="tpu_custom_call" | custom-call | flops 2000000 | bytes 1500000 | tf_op jit(solution)/shard_map/section_outputs/pallas_call | solution.py:465
  106.3 0.6 copy.22
  107.0 0.6 copy.23
  (13 shorter events, 0.0 us)
Async XLA Ops:
  0.6 13.8 %collective-permute-start = (bf16[256,128]{1,0:T(8,128)(2,1)}, bf16[256,128]{1,0:T(8,128)(2,1)S(1)}, u32[]{:S(2)}, u32[]{:S(2)}) collective-permute-start(bf16[256,128]{1,0:T(8,128)(2,1)} %bitcast.29), channel_id=1, source_target_pairs={{0,32},{32,64},{64,96},{96,128},{128,160},{160,192},{192,224},{224... | collective-permute-start | bytes 196616 | tf_op jit(solution)/shard_map/ppermute | solution.py:24
  15.8 8.8 %copy-start = (bf16[1,4,64,2048]{3,2,1,0:T(8,128)(2,1)S(1)}, bf16[1,4,64,2048]{3,2,1,0:T(8,128)(2,1)}, u32[]{:S(2)}) copy-start(bf16[1,4,64,2048]{3,2,1,0:T(8,128)(2,1)} %param.14) | copy-start | bytes 3145732
  15.8 8.8 %copy-start.3 = (s32[1,4,32]{2,1,0:T(4,128)S(1)}, s32[1,4,32]{2,1,0:T(4,128)}, u32[]{:S(2)}) copy-start(s32[1,4,32]{2,1,0:T(4,128)} %param.16) | copy-start | bytes 1540
  15.8 8.8 %copy-start.4 = (s32[1,4,32]{2,1,0:T(4,128)S(1)}, s32[1,4,32]{2,1,0:T(4,128)}, u32[]{:S(2)}) copy-start(s32[1,4,32]{2,1,0:T(4,128)} %param.17) | copy-start | bytes 1540
  15.8 38.5 %all-to-all-start = ((bf16[32,272,128]{2,1,0:T(8,128)(2,1)}), bf16[32,272,128]{2,1,0:T(8,128)(2,1)S(1)}, u32[]{:S(2)}, u32[]{:S(2)}) async-start(bf16[32,272,128]{2,1,0:T(8,128)(2,1)} %pack_base.1.after_ref.spent_ref), calls=%async_computation | async-start | bytes 4456448 | tf_op jit(solution)/shard_map/all_to_all | solution.py:37
  24.6 1.2 %copy-start.1 = (bf16[1,4,64,2048]{3,2,1,0:T(8,128)(2,1)S(1)}, bf16[1,4,64,2048]{3,2,1,0:T(8,128)(2,1)}, u32[]{:S(2)}) copy-start(bf16[1,4,64,2048]{3,2,1,0:T(8,128)(2,1)} %param.15) | copy-start | bytes 3145732
  25.8 14.1 %copy-start.2 = (bf16[1,256,128]{2,1,0:T(8,128)(2,1)S(1)}, bf16[1,256,128]{2,1,0:T(8,128)(2,1)}, u32[]{:S(2)}) copy-start(bf16[1,256,128]{2,1,0:T(8,128)(2,1)} %param.11) | copy-start | bytes 196612
  35.6 18.7 %collective-permute-start.2 = (bf16[256,4096]{1,0:T(8,128)(2,1)}, bf16[256,4096]{1,0:T(8,128)(2,1)}, u32[]{:S(2)}, u32[]{:S(2)}) collective-permute-start(bf16[256,4096]{1,0:T(8,128)(2,1)} %get-tuple-element.29.own_up), channel_id=1, source_target_pairs={{0,1},{1,0},{2,3},{3,2},{4,5},{5,4},{6,7},{7,6},{8,9},{9,8},{10,11... | collective-permute-start | bytes 6291464 | tf_op jit(solution)/shard_map/ppermute | solution.py:29
  37.7 16.6 %collective-permute-start.3 = (bf16[256,4096]{1,0:T(8,128)(2,1)}, bf16[256,4096]{1,0:T(8,128)(2,1)}, u32[]{:S(2)}, u32[]{:S(2)}) collective-permute-start(bf16[256,4096]{1,0:T(8,128)(2,1)} %get-tuple-element.30.own_down), channel_id=1, source_target_pairs={{0,1},{1,0},{2,3},{3,2},{4,5},{5,4},{6,7},{7,6},{8,9},{9,8},{10,11... | collective-permute-start | bytes 6291464 | tf_op jit(solution)/shard_map/ppermute | solution.py:29
  39.9 5.4 %collective-permute-start.1 = (bf16[256,128]{1,0:T(8,128)(2,1)S(1)}, bf16[256,128]{1,0:T(8,128)(2,1)S(1)}, u32[]{:S(2)}, u32[]{:S(2)}) collective-permute-start(bf16[256,128]{1,0:T(8,128)(2,1)S(1)} %broadcast_select_fusion), channel_id=1, source_target_pairs={{0,480},{32,0},{64,32},{96,64},{128,96},{160,128},{192,160},{224,1... | collective-permute-start | bytes 196616 | tf_op jit(solution)/shard_map/ppermute | solution.py:24
  63.1 35.1 %all-to-all-start.1 = ((bf16[32,272,128]{2,1,0:T(8,128)(2,1)}), bf16[32,272,128]{2,1,0:T(8,128)(2,1)}, u32[]{:S(2)}, u32[]{:S(2)}) async-start(bf16[32,272,128]{2,1,0:T(8,128)(2,1)} %get-tuple-element.37), calls=%async_computation.1 | async-start | bytes 4456448 | tf_op jit(solution)/shard_map/all_to_all | solution.py:37
  68.4 4.6 %copy-start.6 = (bf16[1,256,128]{2,1,0:T(8,128)(2,1)S(1)}, bf16[1,256,128]{2,1,0:T(8,128)(2,1)}, u32[]{:S(2)}) copy-start(bf16[1,256,128]{2,1,0:T(8,128)(2,1)} %param.10) | copy-start | bytes 196612
  68.7 6.3 %collective-permute-start.4 = (bf16[64,128,128]{2,1,0:T(8,128)(2,1)S(1)}, bf16[64,128,128]{2,1,0:T(8,128)(2,1)S(1)}, u32[]{:S(2)}, u32[]{:S(2)}) collective-permute-start(bf16[64,128,128]{2,1,0:T(8,128)(2,1)S(1)} %normalize.1.mine_ref), channel_id=1, source_target_pairs={{0,1},{1,0},{2,3},{3,2},{4,5},{5,4},{6,7},{7,6},{8,9},{9,8},{10,11... | collective-permute-start | bytes 6291464 | tf_op jit(solution)/shard_map/ppermute | solution.py:29
  71.0 4.0 %collective-permute-start.5 = (bf16[4,128,128]{2,1,0:T(8,128)(2,1)S(1)}, bf16[4,128,128]{2,1,0:T(8,128)(2,1)S(1)}, u32[]{:S(2)}, u32[]{:S(2)}) collective-permute-start(bf16[4,128,128]{2,1,0:T(8,128)(2,1)S(1)} %get-tuple-element.33), channel_id=1, source_target_pairs={{0,1},{1,0},{2,3},{3,2},{4,5},{5,4},{6,7},{7,6},{8,9},{9,8},{10,11... | collective-permute-start | bytes 393224 | tf_op jit(solution)/shard_map/ppermute | solution.py:29
  73.0 8.3 %collective-permute-start.6 = (bf16[256,128]{1,0:T(8,128)(2,1)S(1)}, bf16[256,128]{1,0:T(8,128)(2,1)S(1)}, u32[]{:S(2)}, u32[]{:S(2)}) collective-permute-start(bf16[256,128]{1,0:T(8,128)(2,1)S(1)} %bitcast.30), channel_id=1, source_target_pairs={{0,32},{32,64},{64,96},{96,128},{128,160},{160,192},{192,224},{224... | collective-permute-start | bytes 196616 | tf_op jit(solution)/shard_map/ppermute | solution.py:24
  75.0 23.3 %copy-start.5 = (bf16[1,128]{1,0:T(2,128)(2,1)S(1)}, bf16[1,128]{1,0:T(2,128)(2,1)}, u32[]{:S(2)}) copy-start(bf16[1,128]{1,0:T(2,128)(2,1)} %gain_ref.1) | copy-start | bytes 772
  100.2 6.1 %collective-permute-start.7 = (bf16[256,128]{1,0:T(8,128)(2,1)S(1)}, bf16[256,128]{1,0:T(8,128)(2,1)S(1)}, u32[]{:S(2)}, u32[]{:S(2)}) collective-permute-start(bf16[256,128]{1,0:T(8,128)(2,1)S(1)} %get-tuple-element.42), channel_id=1, source_target_pairs={{0,480},{32,0},{64,32},{96,64},{128,96},{160,128},{192,160},{224,1... | collective-permute-start | bytes 196616 | tf_op jit(solution)/shard_map/ppermute | solution.py:24

commit v3 on v2

--- a/solution.py
+++ b/solution.py
@@ -447,30 +447,48 @@
     )(parts, base, gain, cot)
 
 
-def outputs_kernel(odd_ref, parts_ref, base_ref, part_ref, out_base_ref, out_part_ref):
-    count = parts_ref.shape[0]
-    tokens = (parts_ref.shape[1] - EXTRA) // 2
+def outputs_kernel(
+    odd_ref, parts_hbm, base_ref, part_ref, back_part_ref, out_base_ref, out_part_ref, back_part_out, parts, sems
+):
+    count = parts_hbm.shape[0]
+    tokens = (parts_hbm.shape[1] - EXTRA) // 2
+    group = 8
+    loads = []
+    for n in range(count // group):
+        at = pl.ds(n * group, group)
+        loads.append(
+            pltpu.make_async_copy(parts_hbm.at[at, pl.ds(tokens, tokens)], parts.at[at], sems.at[n])
+        )
+        loads[-1].start()
     odd = odd_ref[0].astype(F32)
+    back_part_out[...] = back_part_ref[...]
+    totals = [jnp.zeros((tokens, LANES), F32) for _ in range(2)]
+    for n, load in enumerate(loads):
+        load.wait()
+        for j in range(n * group, (n + 1) * group):
+            totals[j % 2] = totals[j % 2] + parts[j].astype(F32)
     for half in range(2):
-        total = jnp.zeros((tokens, LANES), F32)
-        for j in range(half, count, 2):
-            total = total + parts_ref[j, tokens : 2 * tokens, :].astype(F32)
         at = pl.ds(half * tokens, tokens)
         part = part_ref[at, :].astype(F32)
-        out_base_ref[at, :] = (base_ref[at, :].astype(F32) + odd * (part + total)).astype(BF16)
-        out_part_ref[at, :] = ((1.0 - odd) * total).astype(BF16)
-
-
-def outputs(odd, parts, base, part):
+        out_base_ref[at, :] = (base_ref[at, :].astype(F32) + odd * (part + totals[half])).astype(BF16)
+        out_part_ref[at, :] = ((1.0 - odd) * totals[half]).astype(BF16)
+
+
+def outputs(odd, parts, base, part, back_part):
+    count, rows, _ = parts.shape
     return pl.pallas_call(
         outputs_kernel,
-        out_shape=(jax.ShapeDtypeStruct(base.shape, BF16), jax.ShapeDtypeStruct(base.shape, BF16)),
-        in_specs=[SMEM, VMEM, VMEM, VMEM],
-        out_specs=[VMEM] * 2,
+        out_shape=[jax.ShapeDtypeStruct(base.shape, BF16)] * 3,
+        in_specs=[SMEM, HBM, VMEM, VMEM, VMEM],
+        out_specs=[VMEM] * 3,
+        scratch_shapes=[
+            pltpu.VMEM((count, (rows - EXTRA) // 2, LANES), BF16),
+            pltpu.SemaphoreType.DMA((count // 8,)),
+        ],
         compiler_params=PARAMS,
         cost_estimate=pl.CostEstimate(flops=2_000_000, bytes_accessed=1_500_000, transcendentals=0),
         name="section_outputs",
-    )(odd[None], parts, base, part)
+    )(odd[None], parts, base, part, back_part)
 
 
 def per_device(
@@ -512,12 +530,14 @@
         (up_grad, down_grad, arrived_part, part_rows)
     )
     base_gradient, gain_gradient = finish(part_rows, arrived_base, norm_gain, cot_base[0], width)
-    back_base = passed_along(base_gradient, "pipe", -1)
-    out_base, out_part = outputs(odd, part_rows, arrived_base, arrived_part)
+    back_base = passed_along(base_gradient[None], "pipe", -1)
+    out_base, out_part, back_part = outputs(
+        odd, part_rows, arrived_base, arrived_part, back_part
+    )
     return (
         out_base[None],
         out_part[None],
-        back_base[None],
+        back_base,
         back_part[None],
         up_grad[None],
         down_grad[None],

time: 108 us -> 107 us (level)
    unnamed x16 -> x15, local copies, waits for them, and re-layouts: 2.51 us -> 1.89 us
  transfers between devices with their start and end apart: 10 -> 10, of which waited for: 4 -> 4; matrix products, arithmetic and copies ran while one was open for 0% -> 0% of each run, Pallas kernels for 20% -> 19%
where the time goes in v3:
time: 107 us; the launch traced here: 106 us
  starting transfers between devices  36.3 us (34%)
  waiting for transfers between devices  34.8 us (33%)
  Pallas kernels  32.6 us (30%)
  local copies, waits for them, and re-layouts  1.89 us (2%)
    all_to_all x2, waiting for transfers between devices, exchange(): return lax.all_to_all(chunks, 'dp', 0, 0, tiled=True)  25.9 us
    all_to_all x2, starting transfers between devices, exchange(): return lax.all_to_all(chunks, 'dp', 0, 0, tiled=True)  14.1 us
    ppermute x4, starting transfers between devices, passed_along(): lax.ppermute(shard, axis, [(i, (i + by) % count) for i in range(count)])  13.6 us
    pallas_call x1, Pallas kernels, densify(): pl.pallas_call(densify_kernel, out_shape=[jax.ShapeDtypeStruct((hblk * bl...  9.74 us
    ppermute x4, waiting for transfers between devices, passed_along(): lax.ppermute(shard, axis, [(i, (i + by) % count) for i in range(count)])  8.89 us
    pallas_call x1, Pallas kernels, main(): pl.pallas_call(main_kernel, out_shape=(jax.ShapeDtypeStruct(spent.shape,...  8.83 us
    ppermute x4, starting transfers between devices, other_core(): return lax.ppermute(shard, 'dp', [(i, i ^ 1) for i in range(count)])  8.64 us
    pallas_call x1, Pallas kernels, grads(): pl.pallas_call(grads_kernel, out_shape=(jax.ShapeDtypeStruct(shape, BF16)...  6.38 us
  transfers between devices with their start and end apart: 10, of which 4 were waited for; matrix products, arithmetic and copies ran while one was open for 0% of the time, Pallas kernels for 19%

profile of v3, /device:TPU:1, one launch (start us, length us, event | category | flops | bytes accessed | tf_op | source)
XLA Modules:
  0.0 106.5 jit_solution(17839440719227856589)
XLA Ops:
  0.6 4.4 %collective-permute-start = (bf16[256,128]{1,0:T(8,128)(2,1)}, bf16[256,128]{1,0:T(8,128)(2,1)S(1)}, u32[]{:S(2)}, u32[]{:S(2)}) collective-permute-start(bf16[256,128]{1,0:T(8,128)(2,1)} %bitcast.28), channel_id=1, source_target_pairs={{0,32},{32,64},{64,96},{96,128},{128,160},{160,192},{192,224},{224... | collective-permute-start | bytes 196616 | tf_op jit(solution)/shard_map/ppermute | solution.py:24
  5.0 2.2 %pack_cotangent.1.packed_ref = bf16[32,272,128]{2,1,0:T(8,128)(2,1)} custom-call(s32[1]{0:T(128)} %bitcast.odd_ref, bf16[256,128]{1,0:T(8,128)(2,1)} %bitcast.18, bf16[256,128]{1,0:T(8,128)(2,1)} %bitcast.25, bf16[1,128]{1,0:T(2,128)(2,1)} %gain_ref.1), custom_call_target="tpu_custom_call" | custom-call | flops 1000000 | bytes 1500000 | tf_op jit(solution)/shard_map/pack_cotangent/pallas_call | solution.py:72
  7.3 7.2 %collective-permute-done.base_ref = bf16[256,128]{1,0:T(8,128)(2,1)S(1)} collective-permute-done((bf16[256,128]{1,0:T(8,128)(2,1)}, bf16[256,128]{1,0:T(8,128)(2,1)S(1)}, u32[]{:S(2)}, u32[]{:S(2)}) %collective-permute-start) | collective-permute-done | bytes 65568 | tf_op jit(solution)/shard_map/ppermute | solution.py:24
  14.4 1.3 %pack_base.1.after_ref.spent_ref = bf16[32,272,128]{2,1,0:T(8,128)(2,1)} custom-call(bf16[256,128]{1,0:T(8,128)(2,1)S(1)} %collective-permute-done.base_ref, bf16[32,272,128]{2,1,0:T(8,128)(2,1)} %pack_cotangent.1.packed_ref), custom_call_target="tpu_custom_call", output_to_operand_aliasing={{}: (1, {})} | custom-call | flops 1000 | bytes 1000000 | tf_op jit(solution)/shard_map/pack_base/pallas_call | solution.py:108
  15.8 0.0 copy-start
  15.8 0.0 copy-start.3
  15.8 0.0 copy-start.4
  15.8 8.8 %all-to-all-start = ((bf16[32,272,128]{2,1,0:T(8,128)(2,1)}), bf16[32,272,128]{2,1,0:T(8,128)(2,1)S(1)}, u32[]{:S(2)}, u32[]{:S(2)}) async-start(bf16[32,272,128]{2,1,0:T(8,128)(2,1)} %pack_base.1.after_ref.spent_ref), calls=%async_computation | async-start | bytes 4456448 | tf_op jit(solution)/shard_map/all_to_all | solution.py:37
  24.6 0.0 copy-start.1
  24.6 1.2 %copy-done.1 = bf16[1,4,64,2048]{3,2,1,0:T(8,128)(2,1)S(1)} copy-done((bf16[1,4,64,2048]{3,2,1,0:T(8,128)(2,1)S(1)}, bf16[1,4,64,2048]{3,2,1,0:T(8,128)(2,1)}, u32[]{:S(2)}) %copy-start.1) | copy-done | bytes 1048600
  25.8 9.7 %densify.1 = (bf16[256,4096]{1,0:T(8,128)(2,1)}, bf16[256,4096]{1,0:T(8,128)(2,1)}) custom-call(s32[4,32]{1,0:T(4,128)S(1)} %bitcast.20, s32[4,32]{1,0:T(4,128)S(1)} %bitcast.22, bf16[4,64,2048]{2,1,0:T(8,128)(2,1)S(1)} %bitcast.16, bf16[4,64,2048]{2,1,0:T(8,128)(2,1)S(1)} %bitcast.17, bf16[32,272,128]{2,1,0:T(8,128)(2,1)} %pack_base.1.after_ref.spent_ref), custom_call_target="tpu_custom_call" | custom-call | flops 10000000 | bytes 6291456 | tf_op jit(solution)/shard_map/densify/pallas_call | solution.py:170
  35.6 2.1 %collective-permute-start.2 = (bf16[256,4096]{1,0:T(8,128)(2,1)}, bf16[256,4096]{1,0:T(8,128)(2,1)}, u32[]{:S(2)}, u32[]{:S(2)}) collective-permute-start(bf16[256,4096]{1,0:T(8,128)(2,1)} %get-tuple-element.30.own_up), channel_id=1, source_target_pairs={{0,1},{1,0},{2,3},{3,2},{4,5},{5,4},{6,7},{7,6},{8,9},{9,8},{10,11... | collective-permute-start | bytes 6291464 | tf_op jit(solution)/shard_map/ppermute | solution.py:29
  37.7 2.2 %collective-permute-start.3 = (bf16[256,4096]{1,0:T(8,128)(2,1)}, bf16[256,4096]{1,0:T(8,128)(2,1)}, u32[]{:S(2)}, u32[]{:S(2)}) collective-permute-start(bf16[256,4096]{1,0:T(8,128)(2,1)} %get-tuple-element.31.own_down), channel_id=1, source_target_pairs={{0,1},{1,0},{2,3},{3,2},{4,5},{5,4},{6,7},{7,6},{8,9},{9,8},{10,11... | collective-permute-start | bytes 6291464 | tf_op jit(solution)/shard_map/ppermute | solution.py:29
  39.9 3.6 %collective-permute-start.1 = (bf16[256,128]{1,0:T(8,128)(2,1)S(1)}, bf16[256,128]{1,0:T(8,128)(2,1)S(1)}, u32[]{:S(2)}, u32[]{:S(2)}) collective-permute-start(bf16[256,128]{1,0:T(8,128)(2,1)S(1)} %broadcast_select_fusion), channel_id=1, source_target_pairs={{0,480},{32,0},{64,32},{96,64},{128,96},{160,128},{192,160},{224,1... | collective-permute-start | bytes 196616 | tf_op jit(solution)/shard_map/ppermute | solution.py:24
  43.6 1.7 %collective-permute-done.1.back_part_ref = bf16[256,128]{1,0:T(8,128)(2,1)S(1)} collective-permute-done((bf16[256,128]{1,0:T(8,128)(2,1)S(1)}, bf16[256,128]{1,0:T(8,128)(2,1)S(1)}, u32[]{:S(2)}, u32[]{:S(2)}) %collective-permute-start.1) | collective-permute-done | bytes 65568 | tf_op jit(solution)/shard_map/ppermute | solution.py:24
  45.3 9.0 %all-to-all-done.rows_ref = bf16[32,272,128]{2,1,0:T(8,128)(2,1)S(1)} async-done(((bf16[32,272,128]{2,1,0:T(8,128)(2,1)}), bf16[32,272,128]{2,1,0:T(8,128)(2,1)S(1)}, u32[]{:S(2)}, u32[]{:S(2)}) %all-to-all-start) | async-done | bytes 2228256 | tf_op jit(solution)/shard_map/all_to_all | solution.py:37
  54.3 8.8 %forward_backward.1 = (bf16[32,272,128]{2,1,0:T(8,128)(2,1)}, f32[128,128]{1,0:T(8,128)S(1)}, bf16[4,128,128]{2,1,0:T(8,128)(2,1)S(1)}, bf16[4,128,128]{2,1,0:T(8,128)(2,1)S(1)}) custom-call(bf16[32,272,128]{2,1,0:T(8,128)(2,1)S(1)} %all-to-all-done.rows_ref, bf16[256,4096]{1,0:T(8,128)(2,1)} %get-tuple-element.30.own_up, ...), custom_call_target="tpu_custom_call", output_to_operand_aliasing={{0}: (5, {})} | custom-call | flops 2200000000 | bytes 16000000 | tf_op jit(solution)/shard_map/forward_backward/pallas_call | solution.py:273
  63.1 5.3 %all-to-all-start.1 = ((bf16[32,272,128]{2,1,0:T(8,128)(2,1)}), bf16[32,272,128]{2,1,0:T(8,128)(2,1)}, u32[]{:S(2)}, u32[]{:S(2)}) async-start(bf16[32,272,128]{2,1,0:T(8,128)(2,1)} %get-tuple-element.38), calls=%async_computation.1 | async-start | bytes 4456448 | tf_op jit(solution)/shard_map/all_to_all | solution.py:37
  68.4 0.0 copy-start.6
  68.4 0.3 normalize.1.mine_ref
  68.7 2.3 %collective-permute-start.4 = (bf16[64,128,128]{2,1,0:T(8,128)(2,1)S(1)}, bf16[64,128,128]{2,1,0:T(8,128)(2,1)S(1)}, u32[]{:S(2)}, u32[]{:S(2)}) collective-permute-start(bf16[64,128,128]{2,1,0:T(8,128)(2,1)S(1)} %normalize.1.mine_ref), channel_id=1, source_target_pairs={{0,1},{1,0},{2,3},{3,2},{4,5},{5,4},{6,7},{7,6},{8,9},{9,8},{10,11... | collective-permute-start | bytes 6291464 | tf_op jit(solution)/shard_map/ppermute | solution.py:29
  71.0 2.0 %collective-permute-start.5 = (bf16[4,128,128]{2,1,0:T(8,128)(2,1)S(1)}, bf16[4,128,128]{2,1,0:T(8,128)(2,1)S(1)}, u32[]{:S(2)}, u32[]{:S(2)}) collective-permute-start(bf16[4,128,128]{2,1,0:T(8,128)(2,1)S(1)} %get-tuple-element.34), channel_id=1, source_target_pairs={{0,1},{1,0},{2,3},{3,2},{4,5},{5,4},{6,7},{7,6},{8,9},{9,8},{10,11... | collective-permute-start | bytes 393224 | tf_op jit(solution)/shard_map/ppermute | solution.py:29
  73.0 1.9 %collective-permute-start.6 = (bf16[256,128]{1,0:T(8,128)(2,1)S(1)}, bf16[256,128]{1,0:T(8,128)(2,1)S(1)}, u32[]{:S(2)}, u32[]{:S(2)}) collective-permute-start(bf16[256,128]{1,0:T(8,128)(2,1)S(1)} %bitcast.29), channel_id=1, source_target_pairs={{0,32},{32,64},{64,96},{96,128},{128,160},{160,192},{192,224},{224... | collective-permute-start | bytes 196616 | tf_op jit(solution)/shard_map/ppermute | solution.py:24
  75.0 0.0 collective-permute-done.5.given_ref
  75.0 0.0 copy-start.5
  75.0 6.4 %weight_gradients.1 = (bf16[4,64,2048]{2,1,0:T(8,128)(2,1)}, bf16[4,64,2048]{2,1,0:T(8,128)(2,1)}) custom-call(s32[4,32]{1,0:T(4,128)S(1)} %bitcast.21, s32[4,32]{1,0:T(4,128)S(1)} %bitcast.23, bf16[64,128,128]{2,1,0:T(8,128)(2,1)S(1)} %normalize.1.mine_ref, bf16[4,128,128]{2,1,0:T(8,128)(2,1)S(1)} %get-tuple-element.33.keep_ref, ...), custom_call_target="tpu_custom_call" | custom-call | flops 1000000 | bytes 100000 | tf_op jit(solution)/shard_map/weight_gradients/pallas_call | solution.py:372
  81.4 0.0 collective-permute-done.6.part_ref
  81.4 16.9 %all-to-all-done.1.parts_hbm = bf16[32,272,128]{2,1,0:T(8,128)(2,1)} async-done(((bf16[32,272,128]{2,1,0:T(8,128)(2,1)}), bf16[32,272,128]{2,1,0:T(8,128)(2,1)}, u32[]{:S(2)}, u32[]{:S(2)}) %all-to-all-start.1) | async-done | bytes 2228256 | tf_op jit(solution)/shard_map/all_to_all | solution.py:37
  98.3 1.9 %input_gradient.1 = (bf16[256,128]{1,0:T(8,128)(2,1)S(1)}, f32[1,128]{1,0:T(1,128)}) custom-call(bf16[32,272,128]{2,1,0:T(8,128)(2,1)} %all-to-all-done.1.parts_hbm, bf16[256,128]{1,0:T(8,128)(2,1)S(1)} %collective-permute-done.base_ref, bf16[1,128]{1,0:T(2,128)(2,1)S(1)} %copy-done.5, bf16[256,128]{1,0:T(8,128)(2,1)S(1)} %bitcast.19), custom_call_target="tpu_custom_call" | custom-call | flops 2000000 | bytes 1500000 | tf_op jit(solution)/shard_map/input_gradient/pallas_call | solution.py:431
  100.2 3.6 %collective-permute-start.7 = (bf16[1,256,128]{2,1,0:T(8,128)(2,1)S(1)}, bf16[1,256,128]{2,1,0:T(8,128)(2,1)S(1)}, u32[]{:S(2)}, u32[]{:S(2)}) collective-permute-start(bf16[1,256,128]{2,1,0:T(8,128)(2,1)S(1)} %bitcast.24), channel_id=1, source_target_pairs={{0,480},{32,0},{64,32},{96,64},{128,96},{160,128},{192,160},{224,1... | collective-permute-start | bytes 196616 | tf_op jit(solution)/shard_map/ppermute | solution.py:24
  103.9 1.9 %section_outputs.1 = (bf16[256,128]{1,0:T(8,128)(2,1)}, bf16[256,128]{1,0:T(8,128)(2,1)}, bf16[256,128]{1,0:T(8,128)(2,1)}) custom-call(s32[1]{0:T(128)} %bitcast.odd_ref, bf16[32,272,128]{2,1,0:T(8,128)(2,1)} %all-to-all-done.1.parts_hbm, bf16[256,128]{1,0:T(8,128)(2,1)S(1)} %collective-permute-done.base_ref, ...), custom_call_target="tpu_custom_call" | custom-call | flops 2000000 | bytes 1500000 | tf_op jit(solution)/shard_map/section_outputs/pallas_call | solution.py:479
  105.8 0.6 copy.21
  (12 shorter events, 0.0 us)
Async XLA Ops:
  0.6 13.8 %collective-permute-start = (bf16[256,128]{1,0:T(8,128)(2,1)}, bf16[256,128]{1,0:T(8,128)(2,1)S(1)}, u32[]{:S(2)}, u32[]{:S(2)}) collective-permute-start(bf16[256,128]{1,0:T(8,128)(2,1)} %bitcast.28), channel_id=1, source_target_pairs={{0,32},{32,64},{64,96},{96,128},{128,160},{160,192},{192,224},{224... | collective-permute-start | bytes 196616 | tf_op jit(solution)/shard_map/ppermute | solution.py:24
  15.8 8.8 %copy-start = (bf16[1,4,64,2048]{3,2,1,0:T(8,128)(2,1)S(1)}, bf16[1,4,64,2048]{3,2,1,0:T(8,128)(2,1)}, u32[]{:S(2)}) copy-start(bf16[1,4,64,2048]{3,2,1,0:T(8,128)(2,1)} %param.14) | copy-start | bytes 3145732
  15.8 8.8 %copy-start.3 = (s32[1,4,32]{2,1,0:T(4,128)S(1)}, s32[1,4,32]{2,1,0:T(4,128)}, u32[]{:S(2)}) copy-start(s32[1,4,32]{2,1,0:T(4,128)} %param.16) | copy-start | bytes 1540
  15.8 8.8 %copy-start.4 = (s32[1,4,32]{2,1,0:T(4,128)S(1)}, s32[1,4,32]{2,1,0:T(4,128)}, u32[]{:S(2)}) copy-start(s32[1,4,32]{2,1,0:T(4,128)} %param.17) | copy-start | bytes 1540
  15.8 38.5 %all-to-all-start = ((bf16[32,272,128]{2,1,0:T(8,128)(2,1)}), bf16[32,272,128]{2,1,0:T(8,128)(2,1)S(1)}, u32[]{:S(2)}, u32[]{:S(2)}) async-start(bf16[32,272,128]{2,1,0:T(8,128)(2,1)} %pack_base.1.after_ref.spent_ref), calls=%async_computation | async-start | bytes 4456448 | tf_op jit(solution)/shard_map/all_to_all | solution.py:37
  24.6 1.2 %copy-start.1 = (bf16[1,4,64,2048]{3,2,1,0:T(8,128)(2,1)S(1)}, bf16[1,4,64,2048]{3,2,1,0:T(8,128)(2,1)}, u32[]{:S(2)}) copy-start(bf16[1,4,64,2048]{3,2,1,0:T(8,128)(2,1)} %param.15) | copy-start | bytes 3145732
  25.8 14.1 %copy-start.2 = (bf16[1,256,128]{2,1,0:T(8,128)(2,1)S(1)}, bf16[1,256,128]{2,1,0:T(8,128)(2,1)}, u32[]{:S(2)}) copy-start(bf16[1,256,128]{2,1,0:T(8,128)(2,1)} %param.11) | copy-start | bytes 196612
  35.6 18.7 %collective-permute-start.2 = (bf16[256,4096]{1,0:T(8,128)(2,1)}, bf16[256,4096]{1,0:T(8,128)(2,1)}, u32[]{:S(2)}, u32[]{:S(2)}) collective-permute-start(bf16[256,4096]{1,0:T(8,128)(2,1)} %get-tuple-element.30.own_up), channel_id=1, source_target_pairs={{0,1},{1,0},{2,3},{3,2},{4,5},{5,4},{6,7},{7,6},{8,9},{9,8},{10,11... | collective-permute-start | bytes 6291464 | tf_op jit(solution)/shard_map/ppermute | solution.py:29
  37.7 16.6 %collective-permute-start.3 = (bf16[256,4096]{1,0:T(8,128)(2,1)}, bf16[256,4096]{1,0:T(8,128)(2,1)}, u32[]{:S(2)}, u32[]{:S(2)}) collective-permute-start(bf16[256,4096]{1,0:T(8,128)(2,1)} %get-tuple-element.31.own_down), channel_id=1, source_target_pairs={{0,1},{1,0},{2,3},{3,2},{4,5},{5,4},{6,7},{7,6},{8,9},{9,8},{10,11... | collective-permute-start | bytes 6291464 | tf_op jit(solution)/shard_map/ppermute | solution.py:29
  39.9 5.4 %collective-permute-start.1 = (bf16[256,128]{1,0:T(8,128)(2,1)S(1)}, bf16[256,128]{1,0:T(8,128)(2,1)S(1)}, u32[]{:S(2)}, u32[]{:S(2)}) collective-permute-start(bf16[256,128]{1,0:T(8,128)(2,1)S(1)} %broadcast_select_fusion), channel_id=1, source_target_pairs={{0,480},{32,0},{64,32},{96,64},{128,96},{160,128},{192,160},{224,1... | collective-permute-start | bytes 196616 | tf_op jit(solution)/shard_map/ppermute | solution.py:24
  63.1 35.1 %all-to-all-start.1 = ((bf16[32,272,128]{2,1,0:T(8,128)(2,1)}), bf16[32,272,128]{2,1,0:T(8,128)(2,1)}, u32[]{:S(2)}, u32[]{:S(2)}) async-start(bf16[32,272,128]{2,1,0:T(8,128)(2,1)} %get-tuple-element.38), calls=%async_computation.1 | async-start | bytes 4456448 | tf_op jit(solution)/shard_map/all_to_all | solution.py:37
  68.4 4.6 %copy-start.6 = (bf16[1,256,128]{2,1,0:T(8,128)(2,1)S(1)}, bf16[1,256,128]{2,1,0:T(8,128)(2,1)}, u32[]{:S(2)}) copy-start(bf16[1,256,128]{2,1,0:T(8,128)(2,1)} %param.10) | copy-start | bytes 196612
  68.7 6.3 %collective-permute-start.4 = (bf16[64,128,128]{2,1,0:T(8,128)(2,1)S(1)}, bf16[64,128,128]{2,1,0:T(8,128)(2,1)S(1)}, u32[]{:S(2)}, u32[]{:S(2)}) collective-permute-start(bf16[64,128,128]{2,1,0:T(8,128)(2,1)S(1)} %normalize.1.mine_ref), channel_id=1, source_target_pairs={{0,1},{1,0},{2,3},{3,2},{4,5},{5,4},{6,7},{7,6},{8,9},{9,8},{10,11... | collective-permute-start | bytes 6291464 | tf_op jit(solution)/shard_map/ppermute | solution.py:29
  71.0 4.0 %collective-permute-start.5 = (bf16[4,128,128]{2,1,0:T(8,128)(2,1)S(1)}, bf16[4,128,128]{2,1,0:T(8,128)(2,1)S(1)}, u32[]{:S(2)}, u32[]{:S(2)}) collective-permute-start(bf16[4,128,128]{2,1,0:T(8,128)(2,1)S(1)} %get-tuple-element.34), channel_id=1, source_target_pairs={{0,1},{1,0},{2,3},{3,2},{4,5},{5,4},{6,7},{7,6},{8,9},{9,8},{10,11... | collective-permute-start | bytes 393224 | tf_op jit(solution)/shard_map/ppermute | solution.py:29
  73.0 8.3 %collective-permute-start.6 = (bf16[256,128]{1,0:T(8,128)(2,1)S(1)}, bf16[256,128]{1,0:T(8,128)(2,1)S(1)}, u32[]{:S(2)}, u32[]{:S(2)}) collective-permute-start(bf16[256,128]{1,0:T(8,128)(2,1)S(1)} %bitcast.29), channel_id=1, source_target_pairs={{0,32},{32,64},{64,96},{96,128},{128,160},{160,192},{192,224},{224... | collective-permute-start | bytes 196616 | tf_op jit(solution)/shard_map/ppermute | solution.py:24
  75.0 23.3 %copy-start.5 = (bf16[1,128]{1,0:T(2,128)(2,1)S(1)}, bf16[1,128]{1,0:T(2,128)(2,1)}, u32[]{:S(2)}) copy-start(bf16[1,128]{1,0:T(2,128)(2,1)} %gain_ref.1) | copy-start | bytes 772
  100.2 5.6 %collective-permute-start.7 = (bf16[1,256,128]{2,1,0:T(8,128)(2,1)S(1)}, bf16[1,256,128]{2,1,0:T(8,128)(2,1)S(1)}, u32[]{:S(2)}, u32[]{:S(2)}) collective-permute-start(bf16[1,256,128]{2,1,0:T(8,128)(2,1)S(1)} %bitcast.24), channel_id=1, source_target_pairs={{0,480},{32,0},{64,32},{96,64},{128,96},{160,128},{192,160},{224,1... | collective-permute-start | bytes 196616 | tf_op jit(solution)/shard_map/ppermute | solution.py:24

commit v4 on v3

--- a/solution.py
+++ b/solution.py
@@ -56,10 +56,10 @@
         at = pl.ds(n * half, half)
         chunk[n, :half, :] = jnp.where(odd, cot_base_ref[at, :], cot_part_ref[at, :])
         chunk[n, half:, :] = jnp.broadcast_to(gain_ref[...].astype(F32), (EXTRA, LANES)).astype(BF16)
-    for j in range(count):
+    for j in range(count // 2):
         copies.append(
             pltpu.make_async_copy(
-                chunk.at[j % 2], out_ref.at[j, pl.ds(half, half + EXTRA)], sems.at[j]
+                chunk, out_ref.at[pl.ds(2 * j, 2), pl.ds(half, half + EXTRA)], sems.at[j]
             )
         )
         copies[-1].start()
@@ -90,12 +90,12 @@
 
 def pack_base_kernel(base_ref, packed_ref, out_ref, sems):
     count = out_ref.shape[0]
-    half = base_ref.shape[0] // 2
+    halves, half, _ = base_ref.shape
     copies = []
-    for j in range(count):
+    for j in range(count // halves):
         copies.append(
             pltpu.make_async_copy(
-                base_ref.at[pl.ds((j % 2) * half, half)], out_ref.at[j, pl.ds(0, half)], sems.at[j]
+                base_ref, out_ref.at[pl.ds(j * halves, halves), pl.ds(0, half)], sems.at[j]
             )
         )
         copies[-1].start()
@@ -115,7 +115,7 @@
         compiler_params=pltpu.CompilerParams(vmem_limit_bytes=16 * 1024 * 1024),
         cost_estimate=pl.CostEstimate(flops=1_000, bytes_accessed=1_000_000, transcendentals=0),
         name="pack_base",
-    )(base, packed)
+    )(base.reshape(2, -1, LANES), packed)
 
 
 def merge_tiles(tile0, tile1, turned0, turned1, kept0, kept1, lower):
@@ -256,8 +256,8 @@
             j = s // LANES + k
             at = slice(k * LANES, (k + 1) * LANES)
             back_ref[j, :tokens, :] = back[:, at].astype(BF16)
-            back_ref[j, tokens : 2 * tokens, :] = ffn[:, at].astype(BF16)
-            back_ref[j, 2 * tokens :, :] = riding
+            back_ref[j, tokens : tokens + EXTRA, :] = riding
+            back_ref[j, tokens + EXTRA :, :] = ffn[:, at].astype(BF16)
         at = pl.ds(s // LANES, step // LANES)
         stores.append(pltpu.make_async_copy(back_ref.at[at], back_hbm.at[at], out_sems.at[n]))
         stores[-1].start()
@@ -381,39 +381,34 @@
     )(idx_up, idx_down, mine, keep, theirs, given)
 
 
-def finish_kernel(width, parts_hbm, base_ref, gain_ref, cot_ref, out_ref, gain_out_ref, parts, riding_ref, sems):
+def finish_kernel(width, parts_hbm, base_ref, gain_ref, cot_ref, out_ref, gain_out_ref, parts, sems):
     count = parts_hbm.shape[0]
     tokens = (parts_hbm.shape[1] - EXTRA) // 2
     group = 8
-    riding_load = pltpu.make_async_copy(
-        parts_hbm.at[:, pl.ds(2 * tokens, EXTRA)], riding_ref, sems.at[count // group]
-    )
-    riding_load.start()
     loads = []
     for n in range(count // group):
         at = pl.ds(n * group, group)
         loads.append(
-            pltpu.make_async_copy(parts_hbm.at[at, pl.ds(0, tokens)], parts.at[at], sems.at[n])
+            pltpu.make_async_copy(parts_hbm.at[at, pl.ds(0, tokens + EXTRA)], parts.at[at], sems.at[n])
         )
         loads[-1].start()
-    riding_load.wait()
+    totals = [jnp.zeros((tokens, LANES), F32) for _ in range(2)]
+    for n, load in enumerate(loads):
+        load.wait()
+        for j in range(n * group, (n + 1) * group):
+            totals[j % 2] = totals[j % 2] + parts[j, :tokens, :].astype(F32)
     row = lax.broadcasted_iota(jnp.int32, (LANES, LANES), 0)
     stats, inverses = [], []
     for half in range(2):
         riding = jnp.zeros((EXTRA, LANES), F32)
         for j in range(half, count, 2):
-            riding = riding + riding_ref[j].astype(F32)
-        first = riding_ref[half].astype(F32)
+            riding = riding + parts[j, tokens:, :].astype(F32)
+        first = parts[half, tokens:, :].astype(F32)
         summed = (riding[0:1] + riding[1:2]) / width
         inverse = first[2:3] + first[3:4] + first[4:5]
         turned = jnp.transpose(jnp.where(row == 0, summed, jnp.where(row == 1, inverse, 0.0)))
         stats.append(turned[:, 0:1])
         inverses.append(turned[:, 1:2])
-    totals = [jnp.zeros((tokens, LANES), F32) for _ in range(2)]
-    for n, load in enumerate(loads):
-        load.wait()
-        for j in range(n * group, (n + 1) * group):
-            totals[j % 2] = totals[j % 2] + parts[j].astype(F32)
     gain = gain_ref[...].astype(F32)
     total_gain = jnp.zeros((1, LANES), F32)
     for half in range(2):
@@ -437,9 +432,8 @@
         in_specs=[HBM, VMEM, VMEM, VMEM],
         out_specs=[VMEM] * 2,
         scratch_shapes=[
-            pltpu.VMEM((count, (rows - EXTRA) // 2, LANES), BF16),
-            pltpu.VMEM((count, EXTRA, LANES), BF16),
-            pltpu.SemaphoreType.DMA((count // 8 + 1,)),
+            pltpu.VMEM((count, (rows + EXTRA) // 2, LANES), BF16),
+            pltpu.SemaphoreType.DMA((count // 8,)),
         ],
         compiler_params=PARAMS,
         cost_estimate=pl.CostEstimate(flops=2_000_000, bytes_accessed=1_500_000, transcendentals=0),
@@ -457,7 +451,7 @@
     for n in range(count // group):
         at = pl.ds(n * group, group)
         loads.append(
-            pltpu.make_async_copy(parts_hbm.at[at, pl.ds(tokens, tokens)], parts.at[at], sems.at[n])
+            pltpu.make_async_copy(parts_hbm.at[at, pl.ds(tokens + EXTRA, tokens)], parts.at[at], sems.at[n])
         )
         loads[-1].start()
     odd = odd_ref[0].astype(F32)

time: 107 us -> 107 us (level)
  no operation moved by 1% of the time
where the time goes in v4:
time: 107 us
  starting transfers between devices  36.3 us (34%)
  waiting for transfers between devices  34.8 us (33%)
  Pallas kernels  32.8 us (31%)
  local copies, waits for them, and re-layouts  1.89 us (2%)
    all_to_all x2, waiting for transfers between devices, exchange(): return lax.all_to_all(chunks, 'dp', 0, 0, tiled=True)  25.9 us
    all_to_all x2, starting transfers between devices, exchange(): return lax.all_to_all(chunks, 'dp', 0, 0, tiled=True)  14.1 us
    ppermute x4, starting transfers between devices, passed_along(): lax.ppermute(shard, axis, [(i, (i + by) % count) for i in range(count)])  13.6 us
    pallas_call x1, Pallas kernels, densify(): pl.pallas_call(densify_kernel, out_shape=[jax.ShapeDtypeStruct((hblk * bl...  9.74 us
    ppermute x4, waiting for transfers between devices, passed_along(): lax.ppermute(shard, axis, [(i, (i + by) % count) for i in range(count)])  8.89 us
    pallas_call x1, Pallas kernels, main(): pl.pallas_call(main_kernel, out_shape=(jax.ShapeDtypeStruct(spent.shape,...  8.83 us
    ppermute x4, starting transfers between devices, other_core(): return lax.ppermute(shard, 'dp', [(i, i ^ 1) for i in range(count)])  8.64 us
    pallas_call x1, Pallas kernels, grads(): pl.pallas_call(grads_kernel, out_shape=(jax.ShapeDtypeStruct(shape, BF16)...  6.38 us
  transfers between devices with their start and end apart: 10, of which 4 were waited for; matrix products, arithmetic and copies ran while one was open for 0% of the time, Pallas kernels for 19%

profile of v4, /device:TPU:1, one launch (start us, length us, event | category | flops | bytes accessed | tf_op | source)
XLA Modules:
  0.0 106.6 jit_solution(17687420515243382578)
XLA Ops:
  0.6 4.4 %collective-permute-start = (bf16[256,128]{1,0:T(8,128)(2,1)}, bf16[256,128]{1,0:T(8,128)(2,1)S(1)}, u32[]{:S(2)}, u32[]{:S(2)}) collective-permute-start(bf16[256,128]{1,0:T(8,128)(2,1)} %bitcast.30), channel_id=1, source_target_pairs={{0,32},{32,64},{64,96},{96,128},{128,160},{160,192},{192,224},{224... | collective-permute-start | bytes 196616 | tf_op jit(solution)/shard_map/ppermute | solution.py:24
  5.0 2.2 %pack_cotangent.1.packed_ref = bf16[32,272,128]{2,1,0:T(8,128)(2,1)} custom-call(s32[1]{0:T(128)} %bitcast.odd_ref, bf16[256,128]{1,0:T(8,128)(2,1)} %bitcast.20, bf16[256,128]{1,0:T(8,128)(2,1)} %bitcast.27, bf16[1,128]{1,0:T(2,128)(2,1)} %gain_ref.1), custom_call_target="tpu_custom_call" | custom-call | flops 1000000 | bytes 1500000 | tf_op jit(solution)/shard_map/pack_cotangent/pallas_call | solution.py:72
  7.3 7.2 %collective-permute-done.base_ref = bf16[256,128]{1,0:T(8,128)(2,1)S(1)} collective-permute-done((bf16[256,128]{1,0:T(8,128)(2,1)}, bf16[256,128]{1,0:T(8,128)(2,1)S(1)}, u32[]{:S(2)}, u32[]{:S(2)}) %collective-permute-start) | collective-permute-done | bytes 65568 | tf_op jit(solution)/shard_map/ppermute | solution.py:24
  14.4 1.3 %pack_base.1.after_ref.spent_ref = bf16[32,272,128]{2,1,0:T(8,128)(2,1)} custom-call(bf16[2,128,128]{2,1,0:T(8,128)(2,1)S(1)} %bitcast.19, bf16[32,272,128]{2,1,0:T(8,128)(2,1)} %pack_cotangent.1.packed_ref), custom_call_target="tpu_custom_call", output_to_operand_aliasing={{}: (1, {})} | custom-call | flops 1000 | bytes 1000000 | tf_op jit(solution)/shard_map/pack_base/pallas_call | solution.py:108
  15.8 0.0 copy-start
  15.8 0.0 copy-start.3
  15.8 0.0 copy-start.4
  15.8 8.8 %all-to-all-start = ((bf16[32,272,128]{2,1,0:T(8,128)(2,1)}), bf16[32,272,128]{2,1,0:T(8,128)(2,1)S(1)}, u32[]{:S(2)}, u32[]{:S(2)}) async-start(bf16[32,272,128]{2,1,0:T(8,128)(2,1)} %pack_base.1.after_ref.spent_ref), calls=%async_computation | async-start | bytes 4456448 | tf_op jit(solution)/shard_map/all_to_all | solution.py:37
  24.6 0.0 copy-start.1
  24.6 1.2 %copy-done.1 = bf16[1,4,64,2048]{3,2,1,0:T(8,128)(2,1)S(1)} copy-done((bf16[1,4,64,2048]{3,2,1,0:T(8,128)(2,1)S(1)}, bf16[1,4,64,2048]{3,2,1,0:T(8,128)(2,1)}, u32[]{:S(2)}) %copy-start.1) | copy-done | bytes 1048600
  25.8 9.7 %densify.1 = (bf16[256,4096]{1,0:T(8,128)(2,1)}, bf16[256,4096]{1,0:T(8,128)(2,1)}) custom-call(s32[4,32]{1,0:T(4,128)S(1)} %bitcast.22, s32[4,32]{1,0:T(4,128)S(1)} %bitcast.24, bf16[4,64,2048]{2,1,0:T(8,128)(2,1)S(1)} %bitcast.17, bf16[4,64,2048]{2,1,0:T(8,128)(2,1)S(1)} %bitcast.18, bf16[32,272,128]{2,1,0:T(8,128)(2,1)} %pack_base.1.after_ref.spent_ref), custom_call_target="tpu_custom_call" | custom-call | flops 10000000 | bytes 6291456 | tf_op jit(solution)/shard_map/densify/pallas_call | solution.py:170
  35.6 2.1 %collective-permute-start.2 = (bf16[256,4096]{1,0:T(8,128)(2,1)}, bf16[256,4096]{1,0:T(8,128)(2,1)}, u32[]{:S(2)}, u32[]{:S(2)}) collective-permute-start(bf16[256,4096]{1,0:T(8,128)(2,1)} %get-tuple-element.30.own_up), channel_id=1, source_target_pairs={{0,1},{1,0},{2,3},{3,2},{4,5},{5,4},{6,7},{7,6},{8,9},{9,8},{10,11... | collective-permute-start | bytes 6291464 | tf_op jit(solution)/shard_map/ppermute | solution.py:29
  37.7 2.2 %collective-permute-start.3 = (bf16[256,4096]{1,0:T(8,128)(2,1)}, bf16[256,4096]{1,0:T(8,128)(2,1)}, u32[]{:S(2)}, u32[]{:S(2)}) collective-permute-start(bf16[256,4096]{1,0:T(8,128)(2,1)} %get-tuple-element.31.own_down), channel_id=1, source_target_pairs={{0,1},{1,0},{2,3},{3,2},{4,5},{5,4},{6,7},{7,6},{8,9},{9,8},{10,11... | collective-permute-start | bytes 6291464 | tf_op jit(solution)/shard_map/ppermute | solution.py:29
  39.9 3.6 %collective-permute-start.1 = (bf16[256,128]{1,0:T(8,128)(2,1)S(1)}, bf16[256,128]{1,0:T(8,128)(2,1)S(1)}, u32[]{:S(2)}, u32[]{:S(2)}) collective-permute-start(bf16[256,128]{1,0:T(8,128)(2,1)S(1)} %broadcast_select_fusion), channel_id=1, source_target_pairs={{0,480},{32,0},{64,32},{96,64},{128,96},{160,128},{192,160},{224,1... | collective-permute-start | bytes 196616 | tf_op jit(solution)/shard_map/ppermute | solution.py:24
  43.6 1.7 %collective-permute-done.1.back_part_ref = bf16[256,128]{1,0:T(8,128)(2,1)S(1)} collective-permute-done((bf16[256,128]{1,0:T(8,128)(2,1)S(1)}, bf16[256,128]{1,0:T(8,128)(2,1)S(1)}, u32[]{:S(2)}, u32[]{:S(2)}) %collective-permute-start.1) | collective-permute-done | bytes 65568 | tf_op jit(solution)/shard_map/ppermute | solution.py:24
  45.3 9.0 %all-to-all-done.rows_ref = bf16[32,272,128]{2,1,0:T(8,128)(2,1)S(1)} async-done(((bf16[32,272,128]{2,1,0:T(8,128)(2,1)}), bf16[32,272,128]{2,1,0:T(8,128)(2,1)S(1)}, u32[]{:S(2)}, u32[]{:S(2)}) %all-to-all-start) | async-done | bytes 2228256 | tf_op jit(solution)/shard_map/all_to_all | solution.py:37
  54.3 8.8 %forward_backward.1 = (bf16[32,272,128]{2,1,0:T(8,128)(2,1)}, f32[128,128]{1,0:T(8,128)S(1)}, bf16[4,128,128]{2,1,0:T(8,128)(2,1)S(1)}, bf16[4,128,128]{2,1,0:T(8,128)(2,1)S(1)}) custom-call(bf16[32,272,128]{2,1,0:T(8,128)(2,1)S(1)} %all-to-all-done.rows_ref, bf16[256,4096]{1,0:T(8,128)(2,1)} %get-tuple-element.30.own_up, ...), custom_call_target="tpu_custom_call", output_to_operand_aliasing={{0}: (5, {})} | custom-call | flops 2200000000 | bytes 16000000 | tf_op jit(solution)/shard_map/forward_backward/pallas_call | solution.py:273
  63.1 5.3 %all-to-all-start.1 = ((bf16[32,272,128]{2,1,0:T(8,128)(2,1)}), bf16[32,272,128]{2,1,0:T(8,128)(2,1)}, u32[]{:S(2)}, u32[]{:S(2)}) async-start(bf16[32,272,128]{2,1,0:T(8,128)(2,1)} %get-tuple-element.38), calls=%async_computation.1 | async-start | bytes 4456448 | tf_op jit(solution)/shard_map/all_to_all | solution.py:37
  68.4 0.0 copy-start.6
  68.4 0.3 normalize.1.mine_ref
  68.7 2.3 %collective-permute-start.4 = (bf16[64,128,128]{2,1,0:T(8,128)(2,1)S(1)}, bf16[64,128,128]{2,1,0:T(8,128)(2,1)S(1)}, u32[]{:S(2)}, u32[]{:S(2)}) collective-permute-start(bf16[64,128,128]{2,1,0:T(8,128)(2,1)S(1)} %normalize.1.mine_ref), channel_id=1, source_target_pairs={{0,1},{1,0},{2,3},{3,2},{4,5},{5,4},{6,7},{7,6},{8,9},{9,8},{10,11... | collective-permute-start | bytes 6291464 | tf_op jit(solution)/shard_map/ppermute | solution.py:29
  71.0 2.0 %collective-permute-start.5 = (bf16[4,128,128]{2,1,0:T(8,128)(2,1)S(1)}, bf16[4,128,128]{2,1,0:T(8,128)(2,1)S(1)}, u32[]{:S(2)}, u32[]{:S(2)}) collective-permute-start(bf16[4,128,128]{2,1,0:T(8,128)(2,1)S(1)} %get-tuple-element.34), channel_id=1, source_target_pairs={{0,1},{1,0},{2,3},{3,2},{4,5},{5,4},{6,7},{7,6},{8,9},{9,8},{10,11... | collective-permute-start | bytes 393224 | tf_op jit(solution)/shard_map/ppermute | solution.py:29
  73.0 1.9 %collective-permute-start.6 = (bf16[256,128]{1,0:T(8,128)(2,1)S(1)}, bf16[256,128]{1,0:T(8,128)(2,1)S(1)}, u32[]{:S(2)}, u32[]{:S(2)}) collective-permute-start(bf16[256,128]{1,0:T(8,128)(2,1)S(1)} %bitcast.31), channel_id=1, source_target_pairs={{0,32},{32,64},{64,96},{96,128},{128,160},{160,192},{192,224},{224... | collective-permute-start | bytes 196616 | tf_op jit(solution)/shard_map/ppermute | solution.py:24
  75.0 0.0 collective-permute-done.5.given_ref
  75.0 0.0 copy-start.5
  75.0 6.4 %weight_gradients.1 = (bf16[4,64,2048]{2,1,0:T(8,128)(2,1)}, bf16[4,64,2048]{2,1,0:T(8,128)(2,1)}) custom-call(s32[4,32]{1,0:T(4,128)S(1)} %bitcast.23, s32[4,32]{1,0:T(4,128)S(1)} %bitcast.25, bf16[64,128,128]{2,1,0:T(8,128)(2,1)S(1)} %normalize.1.mine_ref, bf16[4,128,128]{2,1,0:T(8,128)(2,1)S(1)} %get-tuple-element.33.keep_ref, ...), custom_call_target="tpu_custom_call" | custom-call | flops 1000000 | bytes 100000 | tf_op jit(solution)/shard_map/weight_gradients/pallas_call | solution.py:372
  81.4 0.0 collective-permute-done.6.part_ref
  81.4 16.9 %all-to-all-done.1.parts_hbm = bf16[32,272,128]{2,1,0:T(8,128)(2,1)} async-done(((bf16[32,272,128]{2,1,0:T(8,128)(2,1)}), bf16[32,272,128]{2,1,0:T(8,128)(2,1)}, u32[]{:S(2)}, u32[]{:S(2)}) %all-to-all-start.1) | async-done | bytes 2228256 | tf_op jit(solution)/shard_map/all_to_all | solution.py:37
  98.3 2.1 %input_gradient.1 = (bf16[256,128]{1,0:T(8,128)(2,1)S(1)}, f32[1,128]{1,0:T(1,128)}) custom-call(bf16[32,272,128]{2,1,0:T(8,128)(2,1)} %all-to-all-done.1.parts_hbm, bf16[256,128]{1,0:T(8,128)(2,1)S(1)} %collective-permute-done.base_ref, bf16[1,128]{1,0:T(2,128)(2,1)S(1)} %copy-done.5, bf16[256,128]{1,0:T(8,128)(2,1)S(1)} %bitcast.21), custom_call_target="tpu_custom_call" | custom-call | flops 2000000 | bytes 1500000 | tf_op jit(solution)/shard_map/input_gradient/pallas_call | solution.py:426
  100.4 3.6 %collective-permute-start.7 = (bf16[1,256,128]{2,1,0:T(8,128)(2,1)S(1)}, bf16[1,256,128]{2,1,0:T(8,128)(2,1)S(1)}, u32[]{:S(2)}, u32[]{:S(2)}) collective-permute-start(bf16[1,256,128]{2,1,0:T(8,128)(2,1)S(1)} %bitcast.26), channel_id=1, source_target_pairs={{0,480},{32,0},{64,32},{96,64},{128,96},{160,128},{192,160},{224,1... | collective-permute-start | bytes 196616 | tf_op jit(solution)/shard_map/ppermute | solution.py:24
  104.0 1.9 %section_outputs.1 = (bf16[256,128]{1,0:T(8,128)(2,1)}, bf16[256,128]{1,0:T(8,128)(2,1)}, bf16[256,128]{1,0:T(8,128)(2,1)}) custom-call(s32[1]{0:T(128)} %bitcast.odd_ref, bf16[32,272,128]{2,1,0:T(8,128)(2,1)} %all-to-all-done.1.parts_hbm, bf16[256,128]{1,0:T(8,128)(2,1)S(1)} %collective-permute-done.base_ref, ...), custom_call_target="tpu_custom_call" | custom-call | flops 2000000 | bytes 1500000 | tf_op jit(solution)/shard_map/section_outputs/pallas_call | solution.py:473
  106.0 0.6 copy.21
  (12 shorter events, 0.0 us)
Async XLA Ops:
  0.6 13.8 %collective-permute-start = (bf16[256,128]{1,0:T(8,128)(2,1)}, bf16[256,128]{1,0:T(8,128)(2,1)S(1)}, u32[]{:S(2)}, u32[]{:S(2)}) collective-permute-start(bf16[256,128]{1,0:T(8,128)(2,1)} %bitcast.30), channel_id=1, source_target_pairs={{0,32},{32,64},{64,96},{96,128},{128,160},{160,192},{192,224},{224... | collective-permute-start | bytes 196616 | tf_op jit(solution)/shard_map/ppermute | solution.py:24
  15.8 8.8 %copy-start = (bf16[1,4,64,2048]{3,2,1,0:T(8,128)(2,1)S(1)}, bf16[1,4,64,2048]{3,2,1,0:T(8,128)(2,1)}, u32[]{:S(2)}) copy-start(bf16[1,4,64,2048]{3,2,1,0:T(8,128)(2,1)} %param.14) | copy-start | bytes 3145732
  15.8 8.8 %copy-start.3 = (s32[1,4,32]{2,1,0:T(4,128)S(1)}, s32[1,4,32]{2,1,0:T(4,128)}, u32[]{:S(2)}) copy-start(s32[1,4,32]{2,1,0:T(4,128)} %param.16) | copy-start | bytes 1540
  15.8 8.8 %copy-start.4 = (s32[1,4,32]{2,1,0:T(4,128)S(1)}, s32[1,4,32]{2,1,0:T(4,128)}, u32[]{:S(2)}) copy-start(s32[1,4,32]{2,1,0:T(4,128)} %param.17) | copy-start | bytes 1540
  15.8 38.5 %all-to-all-start = ((bf16[32,272,128]{2,1,0:T(8,128)(2,1)}), bf16[32,272,128]{2,1,0:T(8,128)(2,1)S(1)}, u32[]{:S(2)}, u32[]{:S(2)}) async-start(bf16[32,272,128]{2,1,0:T(8,128)(2,1)} %pack_base.1.after_ref.spent_ref), calls=%async_computation | async-start | bytes 4456448 | tf_op jit(solution)/shard_map/all_to_all | solution.py:37
  24.6 1.2 %copy-start.1 = (bf16[1,4,64,2048]{3,2,1,0:T(8,128)(2,1)S(1)}, bf16[1,4,64,2048]{3,2,1,0:T(8,128)(2,1)}, u32[]{:S(2)}) copy-start(bf16[1,4,64,2048]{3,2,1,0:T(8,128)(2,1)} %param.15) | copy-start | bytes 3145732
  25.8 14.1 %copy-start.2 = (bf16[1,256,128]{2,1,0:T(8,128)(2,1)S(1)}, bf16[1,256,128]{2,1,0:T(8,128)(2,1)}, u32[]{:S(2)}) copy-start(bf16[1,256,128]{2,1,0:T(8,128)(2,1)} %param.11) | copy-start | bytes 196612
  35.6 18.7 %collective-permute-start.2 = (bf16[256,4096]{1,0:T(8,128)(2,1)}, bf16[256,4096]{1,0:T(8,128)(2,1)}, u32[]{:S(2)}, u32[]{:S(2)}) collective-permute-start(bf16[256,4096]{1,0:T(8,128)(2,1)} %get-tuple-element.30.own_up), channel_id=1, source_target_pairs={{0,1},{1,0},{2,3},{3,2},{4,5},{5,4},{6,7},{7,6},{8,9},{9,8},{10,11... | collective-permute-start | bytes 6291464 | tf_op jit(solution)/shard_map/ppermute | solution.py:29
  37.7 16.6 %collective-permute-start.3 = (bf16[256,4096]{1,0:T(8,128)(2,1)}, bf16[256,4096]{1,0:T(8,128)(2,1)}, u32[]{:S(2)}, u32[]{:S(2)}) collective-permute-start(bf16[256,4096]{1,0:T(8,128)(2,1)} %get-tuple-element.31.own_down), channel_id=1, source_target_pairs={{0,1},{1,0},{2,3},{3,2},{4,5},{5,4},{6,7},{7,6},{8,9},{9,8},{10,11... | collective-permute-start | bytes 6291464 | tf_op jit(solution)/shard_map/ppermute | solution.py:29
  39.9 5.4 %collective-permute-start.1 = (bf16[256,128]{1,0:T(8,128)(2,1)S(1)}, bf16[256,128]{1,0:T(8,128)(2,1)S(1)}, u32[]{:S(2)}, u32[]{:S(2)}) collective-permute-start(bf16[256,128]{1,0:T(8,128)(2,1)S(1)} %broadcast_select_fusion), channel_id=1, source_target_pairs={{0,480},{32,0},{64,32},{96,64},{128,96},{160,128},{192,160},{224,1... | collective-permute-start | bytes 196616 | tf_op jit(solution)/shard_map/ppermute | solution.py:24
  63.1 35.1 %all-to-all-start.1 = ((bf16[32,272,128]{2,1,0:T(8,128)(2,1)}), bf16[32,272,128]{2,1,0:T(8,128)(2,1)}, u32[]{:S(2)}, u32[]{:S(2)}) async-start(bf16[32,272,128]{2,1,0:T(8,128)(2,1)} %get-tuple-element.38), calls=%async_computation.1 | async-start | bytes 4456448 | tf_op jit(solution)/shard_map/all_to_all | solution.py:37
  68.4 4.6 %copy-start.6 = (bf16[1,256,128]{2,1,0:T(8,128)(2,1)S(1)}, bf16[1,256,128]{2,1,0:T(8,128)(2,1)}, u32[]{:S(2)}) copy-start(bf16[1,256,128]{2,1,0:T(8,128)(2,1)} %param.10) | copy-start | bytes 196612
  68.7 6.3 %collective-permute-start.4 = (bf16[64,128,128]{2,1,0:T(8,128)(2,1)S(1)}, bf16[64,128,128]{2,1,0:T(8,128)(2,1)S(1)}, u32[]{:S(2)}, u32[]{:S(2)}) collective-permute-start(bf16[64,128,128]{2,1,0:T(8,128)(2,1)S(1)} %normalize.1.mine_ref), channel_id=1, source_target_pairs={{0,1},{1,0},{2,3},{3,2},{4,5},{5,4},{6,7},{7,6},{8,9},{9,8},{10,11... | collective-permute-start | bytes 6291464 | tf_op jit(solution)/shard_map/ppermute | solution.py:29
  71.0 4.0 %collective-permute-start.5 = (bf16[4,128,128]{2,1,0:T(8,128)(2,1)S(1)}, bf16[4,128,128]{2,1,0:T(8,128)(2,1)S(1)}, u32[]{:S(2)}, u32[]{:S(2)}) collective-permute-start(bf16[4,128,128]{2,1,0:T(8,128)(2,1)S(1)} %get-tuple-element.34), channel_id=1, source_target_pairs={{0,1},{1,0},{2,3},{3,2},{4,5},{5,4},{6,7},{7,6},{8,9},{9,8},{10,11... | collective-permute-start | bytes 393224 | tf_op jit(solution)/shard_map/ppermute | solution.py:29
  73.0 8.3 %collective-permute-start.6 = (bf16[256,128]{1,0:T(8,128)(2,1)S(1)}, bf16[256,128]{1,0:T(8,128)(2,1)S(1)}, u32[]{:S(2)}, u32[]{:S(2)}) collective-permute-start(bf16[256,128]{1,0:T(8,128)(2,1)S(1)} %bitcast.31), channel_id=1, source_target_pairs={{0,32},{32,64},{64,96},{96,128},{128,160},{160,192},{192,224},{224... | collective-permute-start | bytes 196616 | tf_op jit(solution)/shard_map/ppermute | solution.py:24
  75.0 23.3 %copy-start.5 = (bf16[1,128]{1,0:T(2,128)(2,1)S(1)}, bf16[1,128]{1,0:T(2,128)(2,1)}, u32[]{:S(2)}) copy-start(bf16[1,128]{1,0:T(2,128)(2,1)} %gain_ref.1) | copy-start | bytes 772
  100.4 5.6 %collective-permute-start.7 = (bf16[1,256,128]{2,1,0:T(8,128)(2,1)S(1)}, bf16[1,256,128]{2,1,0:T(8,128)(2,1)S(1)}, u32[]{:S(2)}, u32[]{:S(2)}) collective-permute-start(bf16[1,256,128]{2,1,0:T(8,128)(2,1)S(1)} %bitcast.26), channel_id=1, source_target_pairs={{0,480},{32,0},{64,32},{96,64},{128,96},{160,128},{192,160},{224,1... | collective-permute-start | bytes 196616 | tf_op jit(solution)/shard_map/ppermute | solution.py:24
